TPU v7x, 128 devices: a whole 4x4x4 slice. The times are simulated.
128 devices in a mesh: grp: 8 (over x, core), seq: 16 (over z, y).
Axes of the slice: x: 4, y: 4, z: 4, core: 2. Of those that a mesh axis runs over, the one named last changes fastest.
Arguments:
- image_queries: bfloat16 [98304, 768], P(('grp', 'seq')), may hold values from -6 to 6
- image_keys: bfloat16 [98304, 768], P(('grp', 'seq')), may hold values from -6 to 6
- image_values: bfloat16 [98304, 768], P(('grp', 'seq')), may hold values from -6 to 6
- cotangent: bfloat16 [98304, 768], P(('grp', 'seq')), may hold values from -6 to 6
- text_keys: bfloat16 [8, 128, 768], P('grp'), may hold values from -6 to 6
- text_values: bfloat16 [8, 128, 768], P('grp'), may hold values from -6 to 6
- text_lengths: int32 [8], P('grp'), may hold values from 32 to 128, as said below
- send_owner: int32 [128, 6], P(('grp', 'seq')), may hold values from 0 to 15, as said below
- recv_source: int32 [128, 6], P(('grp', 'seq')), may hold values from 0 to 15, as said below
- tile_counts: int32 [128, 3], P(('grp', 'seq')), may hold values from 1 to 3, 6 in all within a row
- caption_ids: int32 [128, 3], P(('grp', 'seq')), may hold values from 0 to 7
Outputs:
- attended: bfloat16 [98304, 768], P(('grp', 'seq'))
- grad_queries: bfloat16 [98304, 768], P(('grp', 'seq'))
- grad_keys: bfloat16 [98304, 768], P(('grp', 'seq'))
- grad_values: bfloat16 [98304, 768], P(('grp', 'seq'))
- grad_text_keys: bfloat16 [8, 128, 768], P('grp')
- grad_text_values: bfloat16 [8, 128, 768], P('grp')
Inputs may be any that keep to these rules, and one draw needn't show every extreme that they name: `send_owner`: within one index of grp, each device sends at most one tile to each owner, and every owner receives exactly 6 tiles, one for each slot, consistent with recv_source. Consistent with send_owner: slot r of owner o is filled by the tile of device recv_source[o, r] whose send_owner entry is o. `text_lengths`: each caption has at least a quarter of its tokens live, and some caption has all 128.
All inputs are finite; a program needn't handle non-finite values.
Results may differ from a plain program's by a relative error of at most 0.008.
Values may be sent and summed in bfloat16 or wider, within the bound.
A program may use at most 192 MiB of HBM per device.

v0:
```python
import jax
import jax.numpy as jnp
from jax import lax
from jax.sharding import PartitionSpec as P

HEAD_DIM = 64


def owner_masks(image_tiles, image_captions, caption_lengths, row_count, tile_rows, text_rows):
    image_count = image_tiles.shape[0]
    image_ends = jnp.cumsum(image_tiles) * tile_rows
    position = jnp.arange(row_count, dtype=jnp.int32)
    segment = jnp.sum((position[:, None] >= image_ends[None, :-1]).astype(jnp.int32), axis=1)
    text_image = jnp.arange(image_count * text_rows, dtype=jnp.int32) // text_rows
    text_place = jnp.arange(image_count * text_rows, dtype=jnp.int32) % text_rows
    chosen = (
        image_captions[:, None] == jnp.arange(caption_lengths.shape[0], dtype=jnp.int32)[None, :]
    )
    caption_length = jnp.sum(jnp.where(chosen, caption_lengths[None, :], 0), axis=1)
    text_live = text_place < jnp.repeat(caption_length, text_rows)
    return (segment, text_image, text_live, chosen)


def split_heads(tensor, column, head_span):
    return tensor[:, column : column + head_span].reshape(
        tensor.shape[0], head_span // HEAD_DIM, HEAD_DIM
    )


def probabilities(query_heads, key_heads, visible, score_scale):
    scores = (
        jnp.einsum("qhd,khd->hqk", query_heads, key_heads, preferred_element_type=jnp.float32)
        * score_scale
    )
    scores = jnp.where(visible[None], scores, -jnp.inf)
    weights = jnp.exp(scores - jnp.max(scores, axis=2, keepdims=True))
    return weights / jnp.sum(weights, axis=2, keepdims=True)


def forward_pass(query_rows, key_all, value_all, visibility, score_scale):
    row_count, feature_width = query_rows.shape
    head_span = min(4 * HEAD_DIM, feature_width)
    block_rows = min(512, row_count)
    columns = []
    for column in range(0, feature_width, head_span):
        key_heads = split_heads(key_all, column, head_span)
        value_heads = split_heads(value_all, column, head_span)
        pieces = []
        for first_row in range(0, row_count, block_rows):
            query_heads = split_heads(
                query_rows[first_row : first_row + block_rows], column, head_span
            )
            taken = query_heads.shape[0]
            prob_full = probabilities(
                query_heads, key_heads, visibility(first_row, taken), score_scale
            )
            mixed_rows = jnp.einsum(
                "hqk,khd->qhd",
                prob_full.astype(jnp.bfloat16),
                value_heads,
                preferred_element_type=jnp.float32,
            )
            pieces.append(mixed_rows.reshape(taken, head_span).astype(jnp.bfloat16))
        columns.append(jnp.concatenate(pieces, 0))
    return jnp.concatenate(columns, 1)


def backward_pass(query_rows, key_all, value_all, grad_rows, visibility, score_scale):
    row_count, feature_width = query_rows.shape
    key_count = key_all.shape[0]
    head_span = min(4 * HEAD_DIM, feature_width)
    block_rows = min(512, row_count)
    query_columns, key_columns, value_columns = ([], [], [])
    for column in range(0, feature_width, head_span):
        key_heads = split_heads(key_all, column, head_span)
        value_heads = split_heads(value_all, column, head_span)
        key_sum = jnp.zeros((key_count, head_span // HEAD_DIM, HEAD_DIM), jnp.float32)
        value_sum = jnp.zeros((key_count, head_span // HEAD_DIM, HEAD_DIM), jnp.float32)
        pieces = []
        for first_row in range(0, row_count, block_rows):
            query_heads = split_heads(
                query_rows[first_row : first_row + block_rows], column, head_span
            )
            grad_heads = split_heads(
                grad_rows[first_row : first_row + block_rows], column, head_span
            )
            taken = query_heads.shape[0]
            prob_full = probabilities(
                query_heads, key_heads, visibility(first_row, taken), score_scale
            )
            prob_low = prob_full.astype(jnp.bfloat16)
            grad_prob = jnp.einsum(
                "qhd,khd->hqk", grad_heads, value_heads, preferred_element_type=jnp.float32
            )
            row_total = jnp.sum(prob_full * grad_prob, axis=2, keepdims=True)
            grad_score = (prob_full * (grad_prob - row_total)).astype(jnp.bfloat16)
            grad_block = (
                jnp.einsum(
                    "hqk,khd->qhd", grad_score, key_heads, preferred_element_type=jnp.float32
                )
                * score_scale
            )
            pieces.append(grad_block.reshape(taken, head_span).astype(jnp.bfloat16))
            key_sum = (
                key_sum
                + jnp.einsum(
                    "hqk,qhd->khd", grad_score, query_heads, preferred_element_type=jnp.float32
                )
                * score_scale
            )
            value_sum = value_sum + jnp.einsum(
                "hqk,qhd->khd", prob_low, grad_heads, preferred_element_type=jnp.float32
            )
        query_columns.append(jnp.concatenate(pieces, 0))
        key_columns.append(key_sum.reshape(key_count, head_span))
        value_columns.append(value_sum.reshape(key_count, head_span))
    return (
        jnp.concatenate(query_columns, 1),
        jnp.concatenate(key_columns, 1),
        jnp.concatenate(value_columns, 1),
    )


def body(
    image_queries,
    image_keys,
    image_values,
    cotangent,
    text_keys,
    text_values,
    text_lengths,
    send_owner,
    recv_source,
    tile_counts,
    caption_ids,
):
    peer_count = lax.axis_size("seq")
    tile_count = send_owner.shape[1]
    row_count, feature_width = image_queries.shape
    tile_rows = row_count // tile_count
    score_scale = HEAD_DIM ** (-0.5)
    all_keys, all_values, all_lengths = (
        lax.all_gather(text_keys, "grp", axis=0, tiled=True),
        lax.all_gather(text_values, "grp", axis=0, tiled=True),
        lax.all_gather(text_lengths, "grp", axis=0, tiled=True),
    )
    text_rows = all_keys.shape[1]
    image_count = tile_counts.shape[1]
    peer_ids = jnp.arange(peer_count, dtype=jnp.int32)
    send_pick = (send_owner[0][None, :] == peer_ids[:, None]).astype(jnp.bfloat16)
    recv_pick = (recv_source[0][:, None] == peer_ids[None, :]).astype(jnp.bfloat16)

    def outbound(tensor):
        return jnp.einsum(
            "pt,tnw->pnw",
            send_pick,
            tensor.reshape(tile_count, tile_rows, feature_width),
            preferred_element_type=jnp.float32,
        ).astype(jnp.bfloat16)

    def inbound(tensor):
        placed = jnp.einsum("tp,pnw->tnw", recv_pick, tensor, preferred_element_type=jnp.float32)
        return placed.astype(jnp.bfloat16).reshape(row_count, feature_width)

    came_queries, came_keys, came_values, came_grads = (
        lax.all_to_all(outbound(image_queries), "seq", split_axis=0, concat_axis=0, tiled=True),
        lax.all_to_all(outbound(image_keys), "seq", split_axis=0, concat_axis=0, tiled=True),
        lax.all_to_all(outbound(image_values), "seq", split_axis=0, concat_axis=0, tiled=True),
        lax.all_to_all(outbound(cotangent), "seq", split_axis=0, concat_axis=0, tiled=True),
    )
    owned_grads = inbound(came_grads)
    owned_queries = inbound(came_queries)
    owned_keys = inbound(came_keys)
    owned_values = inbound(came_values)
    segment, text_image, text_live, chosen = owner_masks(
        tile_counts[0], caption_ids[0], all_lengths, row_count, tile_rows, text_rows
    )
    caption_pick = chosen.astype(jnp.bfloat16)
    image_text_keys = jnp.einsum(
        "ic,ctw->itw", caption_pick, all_keys, preferred_element_type=jnp.float32
    )
    image_text_values = jnp.einsum(
        "ic,ctw->itw", caption_pick, all_values, preferred_element_type=jnp.float32
    )
    key_all = jnp.concatenate(
        [owned_keys, image_text_keys.astype(jnp.bfloat16).reshape(-1, feature_width)], 0
    )
    value_all = jnp.concatenate(
        [owned_values, image_text_values.astype(jnp.bfloat16).reshape(-1, feature_width)], 0
    )

    def visibility(first_row, taken_rows):
        query_segment = segment[first_row : first_row + taken_rows]
        image_part = query_segment[:, None] == segment[None, :]
        text_part = (query_segment[:, None] == text_image[None, :]) & text_live[None, :]
        return jnp.concatenate([image_part, text_part], axis=1)

    attended_owned = forward_pass(owned_queries, key_all, value_all, visibility, score_scale)
    grad_query_owned, grad_key_all, grad_value_all = backward_pass(
        owned_queries, key_all, value_all, owned_grads, visibility, score_scale
    )

    def homeward(tensor):
        return jnp.einsum(
            "tp,tnw->pnw",
            recv_pick,
            tensor.reshape(tile_count, tile_rows, feature_width),
            preferred_element_type=jnp.float32,
        ).astype(jnp.bfloat16)

    back_out, back_queries, back_keys, back_values = (
        lax.all_to_all(homeward(attended_owned), "seq", split_axis=0, concat_axis=0, tiled=True),
        lax.all_to_all(homeward(grad_query_owned), "seq", split_axis=0, concat_axis=0, tiled=True),
        lax.all_to_all(
            homeward(grad_key_all[:row_count].astype(jnp.bfloat16)),
            "seq",
            split_axis=0,
            concat_axis=0,
            tiled=True,
        ),
        lax.all_to_all(
            homeward(grad_value_all[:row_count].astype(jnp.bfloat16)),
            "seq",
            split_axis=0,
            concat_axis=0,
            tiled=True,
        ),
    )

    def settle(tensor):
        placed = jnp.einsum("pt,pnw->tnw", send_pick, tensor, preferred_element_type=jnp.float32)
        return placed.astype(jnp.bfloat16).reshape(row_count, feature_width)

    pick_f32 = chosen.astype(jnp.float32)
    best = lax.Precision.HIGHEST
    table_keys = jnp.einsum(
        "ic,itw->ctw",
        pick_f32,
        grad_key_all[row_count:].reshape(image_count, text_rows, feature_width),
        precision=best,
    )
    table_values = jnp.einsum(
        "ic,itw->ctw",
        pick_f32,
        grad_value_all[row_count:].reshape(image_count, text_rows, feature_width),
        precision=best,
    )
    part_keys, part_values = (
        lax.psum_scatter(table_keys, "grp", scatter_dimension=0, tiled=True),
        lax.psum_scatter(table_values, "grp", scatter_dimension=0, tiled=True),
    )
    total_keys, total_values = lax.psum((part_keys, part_values), "seq")
    grad_text_keys = total_keys.astype(jnp.bfloat16)
    grad_text_values = total_values.astype(jnp.bfloat16)
    return (
        settle(back_out),
        settle(back_queries),
        settle(back_keys),
        settle(back_values),
        grad_text_keys,
        grad_text_values,
    )


def solution(mesh):
    return jax.shard_map(
        body,
        mesh=mesh,
        in_specs=(
            P(("grp", "seq"), None),
            P(("grp", "seq"), None),
            P(("grp", "seq"), None),
            P(("grp", "seq"), None),
            P("grp", None, None),
            P("grp", None, None),
            P("grp"),
            P(("grp", "seq"), None),
            P(("grp", "seq"), None),
            P(("grp", "seq"), None),
            P(("grp", "seq"), None),
        ),
        out_specs=(
            P(("grp", "seq"), None),
            P(("grp", "seq"), None),
            P(("grp", "seq"), None),
            P(("grp", "seq"), None),
            P("grp", None, None),
            P("grp", None, None),
        ),
        check_vma=False,
    )
```

profile of v0, /device:TPU:0, one launch (start us, length us, event | category | flops | bytes accessed | tf_op | source)
XLA Modules:
  0.0 668.9 jit_solution(1111069281035937878)
XLA Ops:
  13.3 8.3 %all-to-all-start.1 = ((bf16[16,128,768]{2,1,0:T(8,128)(2,1)}), bf16[16,128,768]{2,1,0:T(8,128)(2,1)}, u32[]{:S(2)}, u32[]{:S(2)}) async-start(bf16[16,128,768]{2,1,0:T(8,128)(2,1)} %copy.161), calls=%async_computation.1 | async-start | bytes 6291456 | tf_op jit(solution)/shard_map/all_to_all | solution.py:166
  25.9 43.3 %all-to-all-done.1 = bf16[16,128,768]{2,1,0:T(8,128)(2,1)} async-done(((bf16[16,128,768]{2,1,0:T(8,128)(2,1)}), bf16[16,128,768]{2,1,0:T(8,128)(2,1)}, u32[]{:S(2)}, u32[]{:S(2)}) %all-to-all-start.1) | async-done | bytes 3145760 | tf_op jit(solution)/shard_map/all_to_all | solution.py:166
  78.7 39.9 %all-to-all-done.2 = bf16[16,128,768]{2,1,0:T(8,128)(2,1)} async-done(((bf16[16,128,768]{2,1,0:T(8,128)(2,1)}), bf16[16,128,768]{2,1,0:T(8,128)(2,1)}, u32[]{:S(2)}, u32[]{:S(2)}) %all-to-all-start.2) | async-done | bytes 3145760 | tf_op jit(solution)/shard_map/all_to_all | solution.py:167
  125.2 9.3 %all-reduce = s32[8]{0:T(128)S(1)} all-reduce(s32[8]{0:T(128)S(1)} %dynamic-update-slice), channel_id=1, replica_groups=mesh['grp'=8,'seq'=16] {'grp'}, use_global_device_ids=true, to_apply=%add | all-reduce | flops 8 | bytes 64
  140.0 24.6 %all-to-all-done.4 = bf16[16,128,768]{2,1,0:T(8,128)(2,1)} async-done(((bf16[16,128,768]{2,1,0:T(8,128)(2,1)}), bf16[16,128,768]{2,1,0:T(8,128)(2,1)}, u32[]{:S(2)}, u32[]{:S(2)}) %all-to-all-start.4) | async-done | bytes 3145760 | tf_op jit(solution)/shard_map/all_to_all | solution.py:169
  197.6 15.2 %all-to-all-done = bf16[16,128,768]{2,1,0:T(8,128)(2,1)} async-done(((bf16[16,128,768]{2,1,0:T(8,128)(2,1)}), bf16[16,128,768]{2,1,0:T(8,128)(2,1)}, u32[]{:S(2)}, u32[]{:S(2)}) %all-to-all-start) | async-done | bytes 3145760 | tf_op jit(solution)/shard_map/all_to_all | solution.py:168
  238.7 6.2 fusion.212
  249.2 5.6 fusion.47
  265.8 5.9 fusion.211
  280.8 5.6 fusion.43
  297.6 6.9 %fusion.213 = (f32[4,512]{1,0:T(4,128)S(1)}, f32[4,512,1152]{2,1,0:T(8,128)}) fusion(pred[512,1152]{1,0:T(8,128)(4,1)} %pad_add_fusion, bf16[512,4,64]{0,2,1:T(8,128)(2,1)S(1)} %bitcast.270, bf16[1152,4,64]{0,2,1:T(8,128)(2,1)S(1)} %bitcast.227), kind=kOutput, calls=%fused_computation.243 | convolution fusion | flops 311428224 | bytes 10887168 | tf_op jit(solution)/shard_map/sub | solution.py:36
  304.5 5.8 fusion.51
  320.2 6.7 %multiply_reduce_fusion.4 = (f32[4,256]{1,0:T(4,128)}, f32[4,256,1152]{2,1,0:T(8,128)}) fusion(f32[4,256]{1,0:T(4,128)S(1)} %get-tuple-element.42, f32[4,256,1152]{2,1,0:T(8,128)} %get-tuple-element.43, bf16[256,4,64]{0,2,1:T(8,128)(2,1)} %bitcast.334, bf16[1152,4,64]{0,2,1:T(8,128)(2,1)} %bitcast.300), kind=kOutput, calls=%fused_computation.33 | convolution fusion | flops 154532864 | bytes 10166272 | tf_op jit(solution)/shard_map/qhd,khd->hqk/dot_general | solution.py:92
  326.9 6.3 multiply_reduce_fusion.3
  333.3 5.5 multiply_reduce_fusion.1
  352.5 5.5 fusion.110
  374.9 8.7 %multiply_reduce_fusion.2 = (f32[4,512]{1,0:T(4,128)}, f32[4,512,1152]{2,1,0:T(8,128)}) fusion(f32[4,512,1152]{2,1,0:T(8,128)} %get-tuple-element.49, f32[4,512]{1,0:T(4,128)S(1)} %get-tuple-element.48, bf16[512,4,64]{0,2,1:T(8,128)(2,1)S(1)} %bitcast.321, bf16[1152,4,64]{0,2,1:T(8,128)(2,1)S(1)} %bitcast.293), kind=kOutput, calls=%fused_computation.11 | convolution fusion | flops 309065728 | bytes 19742720 | tf_op jit(solution)/shard_map/qhd,khd->hqk/dot_general | solution.py:92
  420.4 6.4 multiply_reduce_fusion.5
  427.0 5.9 multiply_convert_fusion.2
  432.9 7.2 %all-to-all-start.3 = ((bf16[16,128,768]{2,1,0:T(8,128)(2,1)}), bf16[16,128,768]{2,1,0:T(8,128)(2,1)}, u32[]{:S(2)}, u32[]{:S(2)}) async-start(bf16[16,128,768]{2,1,0:T(8,128)(2,1)} %copy.189), calls=%async_computation.3 | async-start | bytes 6291456 | tf_op jit(solution)/shard_map/all_to_all | solution.py:212
  467.7 13.0 %all-to-all-done.3 = bf16[16,128,768]{2,1,0:T(8,128)(2,1)} async-done(((bf16[16,128,768]{2,1,0:T(8,128)(2,1)}), bf16[16,128,768]{2,1,0:T(8,128)(2,1)}, u32[]{:S(2)}, u32[]{:S(2)}) %all-to-all-start.3) | async-done | bytes 3145760 | tf_op jit(solution)/shard_map/all_to_all | solution.py:212
  513.8 15.6 %all-to-all-done.6 = bf16[16,128,768]{2,1,0:T(8,128)(2,1)} async-done(((bf16[16,128,768]{2,1,0:T(8,128)(2,1)}), bf16[16,128,768]{2,1,0:T(8,128)(2,1)}, u32[]{:S(2)}, u32[]{:S(2)}) %all-to-all-start.6) | async-done | bytes 3145760 | tf_op jit(solution)/shard_map/all_to_all | solution.py:214
  549.1 27.1 %all-to-all-done.5 = bf16[16,128,768]{2,1,0:T(8,128)(2,1)} async-done(((bf16[16,128,768]{2,1,0:T(8,128)(2,1)}), bf16[16,128,768]{2,1,0:T(8,128)(2,1)}, u32[]{:S(2)}, u32[]{:S(2)}) %all-to-all-start.5) | async-done | bytes 3145760 | tf_op jit(solution)/shard_map/all_to_all | solution.py:213
  581.1 80.8 %all-reduce.3 = (bf16[1,128,768]{2,1,0:T(8,128)(2,1)}, bf16[1,128,768]{2,1,0:T(8,128)(2,1)}) all-reduce(f32[1,128,768]{2,1,0:T(8,128)} %reduce-scatter.3.cloned.1.call-done, f32[1,128,768]{2,1,0:T(8,128)} %reduce-scatter.5.cloned.1.call-done), channel_id=1, replica_groups=mesh['grp'=8,'seq'=16] {'seq'}, use_global_device_ids=true, to_apply=%region_22.23 | all-reduce | flops 196608 | bytes 1179648 | tf_op jit(solution)/shard_map/psum | solution.py:252
  (350 shorter events, 287.6 us)
Async XLA Ops:
  13.3 55.9 %all-to-all-start.1 = ((bf16[16,128,768]{2,1,0:T(8,128)(2,1)}), bf16[16,128,768]{2,1,0:T(8,128)(2,1)}, u32[]{:S(2)}, u32[]{:S(2)}) async-start(bf16[16,128,768]{2,1,0:T(8,128)(2,1)} %copy.161), calls=%async_computation.1 | async-start | bytes 6291456 | tf_op jit(solution)/shard_map/all_to_all | solution.py:166
  25.9 48.5 %copy-start.21 = (bf16[768,768]{1,0:T(8,128)(2,1)S(1)}, bf16[768,768]{1,0:T(8,128)(2,1)}, u32[]{:S(2)}) copy-start(bf16[768,768]{1,0:T(8,128)(2,1)} %param.14) | copy-start | bytes 3538948
  69.2 49.4 %all-to-all-start.2 = ((bf16[16,128,768]{2,1,0:T(8,128)(2,1)}), bf16[16,128,768]{2,1,0:T(8,128)(2,1)}, u32[]{:S(2)}, u32[]{:S(2)}) async-start(bf16[16,128,768]{2,1,0:T(8,128)(2,1)} %copy.166), calls=%async_computation.2 | async-start | bytes 6291456 | tf_op jit(solution)/shard_map/all_to_all | solution.py:167
  73.7 97.4 %all-gather.5.cloned.1.call-start = ((), (), s32[]{:S(2)}) async-start(), calls=%async_computation.11 | async-start | bytes 1769472 | tf_op jit(solution)/shard_map/all_gather | solution.py:143
  78.7 45.1 %copy-start.74 = (u32[128]{0:T(128)S(1)}, u32[128]{0:T(128)}, u32[]{:S(2)}) copy-start(u32[128]{0:T(128)} %constant.55) | copy-start | bytes 1540
  78.7 55.7 %copy-start.73 = (s32[1,3]{1,0:T(1,128)S(1)}, s32[1,3]{1,0:T(1,128)}, u32[]{:S(2)}) copy-start(s32[1,3]{1,0:T(1,128)} %param.20) | copy-start | bytes 40
  78.7 56.0 %copy-start.22 = (bf16[768,768]{1,0:T(8,128)(2,1)S(1)}, bf16[768,768]{1,0:T(8,128)(2,1)}, u32[]{:S(2)}) copy-start(bf16[768,768]{1,0:T(8,128)(2,1)} %param.13) | copy-start | bytes 3538948
  118.6 45.9 %all-to-all-start.4 = ((bf16[16,128,768]{2,1,0:T(8,128)(2,1)}), bf16[16,128,768]{2,1,0:T(8,128)(2,1)}, u32[]{:S(2)}, u32[]{:S(2)}) async-start(bf16[16,128,768]{2,1,0:T(8,128)(2,1)} %copy.193), calls=%async_computation.4 | async-start | bytes 6291456 | tf_op jit(solution)/shard_map/all_to_all | solution.py:169
  123.1 50.6 %all-gather.3.cloned.1.call-start = ((), (), s32[]{:S(2)}) async-start(), calls=%async_computation.10 | async-start | bytes 1769472 | tf_op jit(solution)/shard_map/all_gather | solution.py:144
  164.5 48.3 %all-to-all-start = ((bf16[16,128,768]{2,1,0:T(8,128)(2,1)}), bf16[16,128,768]{2,1,0:T(8,128)(2,1)}, u32[]{:S(2)}, u32[]{:S(2)}) async-start(bf16[16,128,768]{2,1,0:T(8,128)(2,1)} %copy.154), calls=%async_computation | async-start | bytes 6291456 | tf_op jit(solution)/shard_map/all_to_all | solution.py:168
  169.0 412.1 %reduce-scatter.5.cloned.1.call-start = ((), (), s32[]{:S(2)}) async-start(), calls=%async_computation.13 | async-start | bytes 3538944 | tf_op jit(solution)/shard_map/reduce_scatter | solution.py:250
  197.0 113.3 %copy-start.12 = (bf16[1152,256]{0,1:T(8,128)(2,1)}, bf16[1152,256]{0,1:T(8,128)(2,1)S(1)}, u32[]{:S(2)}) copy-start(bf16[1152,256]{0,1:T(8,128)(2,1)S(1)} %copy.171) | copy-start | bytes 1769476
  197.3 89.1 %copy-start.16 = (bf16[1152,256]{0,1:T(8,128)(2,1)}, bf16[1152,256]{0,1:T(8,128)(2,1)S(1)}, u32[]{:S(2)}) copy-start(bf16[1152,256]{0,1:T(8,128)(2,1)S(1)} %copy.184) | copy-start | bytes 1769476
  197.6 57.2 %copy-start.18 = (bf16[1152,256]{0,1:T(8,128)(2,1)}, bf16[1152,256]{0,1:T(8,128)(2,1)S(1)}, u32[]{:S(2)}) copy-start(bf16[1152,256]{0,1:T(8,128)(2,1)S(1)} %copy.178) | copy-start | bytes 1769476
  235.2 85.0 %copy-start.66 = (f32[4,256]{1,0:T(4,128)}, f32[4,256]{1,0:T(4,128)S(1)}, u32[]{:S(2)}) copy-start(f32[4,256]{1,0:T(4,128)S(1)} %get-tuple-element.42) | copy-start | bytes 12292
  265.8 61.1 %copy-start.68 = (f32[4,256]{1,0:T(4,128)}, f32[4,256]{1,0:T(4,128)S(1)}, u32[]{:S(2)}) copy-start(f32[4,256]{1,0:T(4,128)S(1)} %get-tuple-element.38) | copy-start | bytes 12292
  320.1 54.7 %copy-start.30 = (bf16[1152,256]{0,1:T(8,128)(2,1)}, bf16[1152,256]{0,1:T(8,128)(2,1)S(1)}, u32[]{:S(2)}) copy-start(bf16[1152,256]{0,1:T(8,128)(2,1)S(1)} %copy.159) | copy-start | bytes 1769476
  370.0 62.9 %all-to-all-start.7 = ((bf16[16,128,768]{2,1,0:T(8,128)(2,1)}), bf16[16,128,768]{2,1,0:T(8,128)(2,1)}, u32[]{:S(2)}, u32[]{:S(2)}) async-start(bf16[16,128,768]{2,1,0:T(8,128)(2,1)} %copy.224), calls=%async_computation.7 | async-start | bytes 6291456 | tf_op jit(solution)/shard_map/all_to_all | solution.py:221
  432.9 47.9 %all-to-all-start.3 = ((bf16[16,128,768]{2,1,0:T(8,128)(2,1)}), bf16[16,128,768]{2,1,0:T(8,128)(2,1)}, u32[]{:S(2)}, u32[]{:S(2)}) async-start(bf16[16,128,768]{2,1,0:T(8,128)(2,1)} %copy.189), calls=%async_computation.3 | async-start | bytes 6291456 | tf_op jit(solution)/shard_map/all_to_all | solution.py:212
  440.1 141.1 %reduce-scatter.3.cloned.1.call-start = ((), (), s32[]{:S(2)}) async-start(), calls=%async_computation.12 | async-start | bytes 3538944 | tf_op jit(solution)/shard_map/reduce_scatter | solution.py:249
  480.7 48.7 %all-to-all-start.6 = ((bf16[16,128,768]{2,1,0:T(8,128)(2,1)}), bf16[16,128,768]{2,1,0:T(8,128)(2,1)}, u32[]{:S(2)}, u32[]{:S(2)}) async-start(bf16[16,128,768]{2,1,0:T(8,128)(2,1)} %copy.217), calls=%async_computation.6 | async-start | bytes 6291456 | tf_op jit(solution)/shard_map/all_to_all | solution.py:214
  513.8 20.4 %copy-start.55 = (s32[1,6]{1,0:T(1,128)S(1)}, s32[1,6]{1,0:T(1,128)}, u32[]{:S(2)}) copy-start(s32[1,6]{1,0:T(1,128)} %param.18) | copy-start | bytes 76
  529.4 46.7 %all-to-all-start.5 = ((bf16[16,128,768]{2,1,0:T(8,128)(2,1)}), bf16[16,128,768]{2,1,0:T(8,128)(2,1)}, u32[]{:S(2)}, u32[]{:S(2)}) async-start(bf16[16,128,768]{2,1,0:T(8,128)(2,1)} %copy.210), calls=%async_computation.5 | async-start | bytes 6291456 | tf_op jit(solution)/shard_map/all_to_all | solution.py:213
  547.9 114.1 %copy-start.1 = (bf16[768,768]{1,0:T(8,128)(2,1)S(1)}, bf16[768,768]{1,0:T(8,128)(2,1)}, u32[]{:S(2)}) copy-start(bf16[768,768]{1,0:T(8,128)(2,1)} %param.11) | copy-start | bytes 3538948
  (80 other events, 415.7 us)
Sparse Core Ops, SparseCore 0:
  76.2 25.6 all-gather.4
  125.6 25.6 all-gather.2
  364.7 34.1 reduce-scatter.4
  462.4 37.8 reduce-scatter.2
where the time goes:
time: 678 us; the launch traced here: 669 us
  matrix products  211 us (31%)
  waiting for transfers between devices  179 us (26%)
  local copies, waits for them, and re-layouts  96.9 us (14%)
  blocking collectives  90 us (13%)
  starting transfers between devices  43.5 us (6%)
  other arithmetic  31.7 us (5%)
  between operations  16.1 us (2%)
    psum x1, blocking collectives, body(): total_keys, total_values = lax.psum((part_keys, part_values), 'seq')  80.8 us
    all_to_all x1, waiting for transfers between devices, body(): lax.all_to_all(outbound(image_queries), 'seq', split_axis=0, concat_axis=...  43.3 us
    all_to_all x1, waiting for transfers between devices, body(): lax.all_to_all(outbound(image_keys), 'seq', split_axis=0, concat_axis=0,...  39.9 us
    dot_general x6, matrix products, backward_pass(): jnp.einsum('qhd,khd->hqk', grad_heads, value_heads, preferred_element_typ...  36.2 us
    sub x6, matrix products, probabilities(): weights = jnp.exp(scores - jnp.max(scores, axis=2, keepdims=True))  34.1 us
    dot_general x6, matrix products, backward_pass(): jnp.einsum('hqk,qhd->khd', prob_low, grad_heads, preferred_element_type=j...  30.1 us
    all_to_all x1, waiting for transfers between devices, body(): lax.all_to_all(homeward(grad_query_owned), 'seq', split_axis=0, concat_ax...  27.1 us
    dot_general x6, matrix products, forward_pass(): jnp.einsum('hqk,khd->qhd', prob_full.astype(jnp.bfloat16), value_heads, p...  25.9 us
  transfers between devices with their start and end apart: 12, of which 7 were waited for; matrix products, arithmetic and copies ran while one was open for 26% of the time, Pallas kernels for 0%

commit v1 on v0

v1 whole, which is shorter than its diff:
```python
import functools

import jax
import jax.numpy as jnp
from jax import lax
from jax.experimental import pallas as pl
from jax.experimental.pallas import tpu as pltpu
from jax.sharding import PartitionSpec as P

HEAD_DIM = 64
LANES = 128
TILE = 128
MESH = pl.DeviceIdType.MESH

RING = 4
SLOTS = 4
RELAY = 2

OWN = 0
DIRECT = 9
FORWARD = 17
FINAL = 21
PASSING = 29
POOL = 33

P_SEND = 0
P_MID = 8
P_LATE = 16
P_IMAGE = 20
P_BACK = 32
P_BACK_MID = 40
P_BACK_LATE = 48
P_HOME = 52
P_SIZE = 64

T_RECV, T_COUNT, T_CAPTION, T_LENGTH = 6, 12, 15, 18

SEND, PASS, MID, LATE = range(4)


def plan_kernel(tab_ref, row_ref, out_ref):
    g = lax.axis_index("grp")
    me = lax.axis_index("seq")
    peers = 16
    tab = tab_ref[pl.ds(pl.multiple_of(g * peers, peers), peers), :]
    src = lax.broadcasted_iota(jnp.int32, (peers, LANES), 0)
    own = lax.broadcasted_iota(jnp.int32, (peers, LANES), 1)
    sends = jnp.zeros((peers, LANES), jnp.int32)
    place = jnp.zeros((peers, LANES), jnp.int32)
    for j in range(6):
        hit = (tab[:, j : j + 1] == own).astype(jnp.int32)
        sends += hit
        place += hit * j
    first = row_ref[0, T_COUNT]
    second = first + row_ref[0, T_COUNT + 1]
    result = jnp.zeros((peers, LANES), jnp.int32)
    padded = []
    for r in range(6):
        image = jnp.where(r >= first, 1, 0) + jnp.where(r >= second, 1, 0)
        begin = jnp.where(r >= second, second, jnp.where(r >= first, first, 0))
        where_r = image * 3 + r - begin
        padded.append(where_r)
        result += jnp.where(src == row_ref[0, T_RECV + r], where_r, 0)

    lower = (
        lax.broadcasted_iota(jnp.int32, (peers, peers), 1)
        < lax.broadcasted_iota(jnp.int32, (peers, peers), 0)
    ).astype(jnp.float32)
    upper = (
        lax.broadcasted_iota(jnp.int32, (LANES, LANES), 0)
        < lax.broadcasted_iota(jnp.int32, (LANES, LANES), 1)
    ).astype(jnp.float32)
    live = sends > 0
    coord = {"y": lambda t: lax.rem(t, RING), "z": lambda t: lax.div(t, RING) % RING}

    def slots(step, axis):
        count, rank = [], []
        for d in (1, 2, 3):
            picked = jnp.where(live & (step == d), 1.0, 0.0)
            if axis == 1:
                before = jnp.dot(picked, upper, preferred_element_type=jnp.float32)
            else:
                before = jnp.dot(lower, picked, preferred_element_type=jnp.float32)
            rank.append(before.astype(jnp.int32))
            count.append(jnp.sum(picked, axis=axis, keepdims=True).astype(jnp.int32))
        plus = jnp.minimum(jnp.minimum(RELAY, SLOTS - count[0]), count[1])
        code = jnp.where(
            step == 0,
            0,
            jnp.where(
                step == 1, 1, jnp.where(step == 3, 2, jnp.where(rank[1] < plus, 3, 4))
            ),
        )
        slot = jnp.where(
            code == 1,
            SLOTS - 1 - rank[0],
            jnp.where(
                code == 2,
                SLOTS - 1 - rank[2],
                jnp.where(code == 3, rank[1], rank[1] - plus),
            ),
        )
        return code, slot

    def arrived(code, slot, stay, flip):
        base = (DIRECT + SLOTS, DIRECT, FORWARD + RELAY, FORWARD) if flip else (
            DIRECT, DIRECT + SLOTS, FORWARD, FORWARD + RELAY)
        return jnp.where(
            code == 0,
            stay,
            slot
            + jnp.where(
                code == 1,
                base[0],
                jnp.where(code == 2, base[1], jnp.where(code == 3, base[2], base[3])),
            ),
        )

    def settled(code, slot, stay, flip):
        odd = (code == 1) | (code == 3)
        near, far = (FINAL + SLOTS, FINAL) if flip else (FINAL, FINAL + SLOTS)
        return jnp.where(code == 0, stay, slot + jnp.where(odd, near, far))

    zero_row = jnp.zeros((1, LANES), jnp.float32)
    rows = []
    for ring_a, ring_b in (("y", "z"), ("z", "y")):
        at_a, at_b = coord[ring_a], coord[ring_b]
        src_a, src_b, own_a, own_b = at_a(src), at_b(src), at_a(own), at_b(own)
        me_a, me_b = at_a(me), at_b(me)
        code_a, slot_a = slots(lax.rem(own_a - src_a + RING, RING), 1)
        code_b, slot_b = slots(lax.rem(own_b - src_b + RING, RING), 0)
        there = arrived(code_a, slot_a, place, False)
        there_end = settled(code_b, slot_b, there, False)
        back = arrived(code_b, slot_b, result, True)
        back_end = settled(code_a, slot_a, back, True)
        mine_src = live & (src == me)
        mine_own = live & (own == me)
        crossing = live & (own_a == me_a) & (src_b == me_b)
        part = {}

        def put(entry, condition, value):
            row = jnp.sum(
                jnp.where(condition, value, 0).astype(jnp.float32), axis=0, keepdims=True
            )
            part[entry] = part[entry] + row if entry in part else row

        def channel(code, sign, flip):
            sign = 1 - sign if flip else sign
            return (code == 1 + sign), (code == 3 + sign)

        for sign in (0, 1):
            ahead = 1 if sign == 0 else RING - 1
            near, far = channel(code_a, sign, False)
            for k in range(SLOTS):
                put(P_SEND + sign * SLOTS + k, mine_src & (near | far) & (slot_a == k), place)
            near, far = channel(code_b, sign, False)
            passing = live & (own_a == me_a) & far & (lax.rem(own_b - me_b + RING, RING) == ahead)
            for k in range(RELAY):
                put(P_MID + sign * SLOTS + k, crossing & far & (slot_b == k), there)
                put(P_LATE + sign * RELAY + k, crossing & near & (slot_b == k), there)
                put(P_LATE + sign * RELAY + k, passing & (slot_b == k), PASSING + sign * RELAY + k)
            for k in range(RELAY, SLOTS):
                put(P_MID + sign * SLOTS + k, crossing & near & (slot_b == k), there)
            near, far = channel(code_b, sign, True)
            for k in range(SLOTS):
                put(P_BACK + sign * SLOTS + k, mine_own & (near | far) & (slot_b == k), result)
            near, far = channel(code_a, sign, True)
            passing = live & (src_b == me_b) & far & (lax.rem(src_a - me_a + RING, RING) == ahead)
            for k in range(RELAY):
                put(P_BACK_MID + sign * SLOTS + k, crossing & far & (slot_a == k), back)
                put(P_BACK_LATE + sign * RELAY + k, crossing & near & (slot_a == k), back)
                put(P_BACK_LATE + sign * RELAY + k, passing & (slot_a == k), PASSING + sign * RELAY + k)
            for k in range(RELAY, SLOTS):
                put(P_BACK_MID + sign * SLOTS + k, crossing & near & (slot_a == k), back)
        begins = (0, first, second)
        for i in range(3):
            for j in range(3):
                r = jnp.minimum(begins[i] + j, 5)
                put(P_IMAGE + i * 3 + j, mine_own & (src == row_ref[0, T_RECV + r]), there_end)
        for j in range(6):
            put(P_HOME + j, mine_src & (place == j), back_end)
        rows.extend(part.get(entry, zero_row) for entry in range(P_SIZE))
    matrix = jnp.concatenate(rows, axis=0)
    ones = jnp.ones((8, LANES), jnp.float32)
    out = lax.dot_general(ones, matrix, (((1,), (1,)), ((), ())), preferred_element_type=jnp.float32)
    out_ref[...] = out.astype(jnp.int32)


def main_kernel(
    peers_grp,
    pairs,
    plan,
    tab,
    queries,
    keys,
    values,
    grads,
    cap_keys,
    cap_values,
    out_rows,
    out_queries,
    out_keys,
    out_values,
    out_text,
    inb,
    txt,
    send_a,
    recv_a,
    recv_p,
    send_m,
    recv_m,
    send_l,
    recv_l,
    pool,
    res,
    stage,
    tsend,
    trecv,
    ttot,
    ssem,
    rsem,
    tssem,
    trsem,
    insem,
    outsem,
):
    g = lax.axis_index("grp")
    s = lax.axis_index("seq")
    z, y = lax.div(s, RING), lax.rem(s, RING)
    row = g * (RING * RING) + s
    sources = (queries, keys, values, grads)
    outs = (out_rows, out_queries, out_keys, out_values)

    def neighbour(ring, sign):
        step = 1 if sign == 0 else RING - 1
        if ring == "y":
            return (g, z * RING + lax.rem(y + step, RING))
        return (g, lax.rem(z + step, RING) * RING + y)

    def group_peer(k):
        return lax.rem(g + k, peers_grp)

    barrier = pltpu.get_barrier_semaphore()
    for ring in ("y", "z"):
        for sign in (0, 1):
            pl.semaphore_signal(barrier, inc=1, device_id=neighbour(ring, sign), device_id_type=MESH)
    for k in range(1, peers_grp):
        pl.semaphore_signal(barrier, inc=1, device_id=(group_peer(k), s), device_id_type=MESH)

    def message(io, par, ty, sign, kind):
        ring = "y" if (ty + io + (1 if kind >= MID else 0)) % 2 == 0 else "z"
        if kind == SEND:
            src, dst = send_a.at[io, ty, sign], recv_a.at[io, par, ty, sign]
        elif kind == PASS:
            src, dst = recv_a.at[io, par, ty, sign, pl.ds(0, RELAY)], recv_p.at[io, par, ty, sign]
        elif kind == MID:
            src, dst = send_m.at[io, ty, sign], recv_m.at[io, par, ty, sign]
        else:
            src, dst = send_l.at[io, ty, sign], recv_l.at[io, par, ty, sign]
        index = (((io * 2 + par) * 2 + ty) * 2 + sign) * 4 + kind
        return pltpu.make_async_remote_copy(
            src_ref=src,
            dst_ref=dst,
            send_sem=ssem.at[index],
            recv_sem=rsem.at[index],
            device_id=neighbour(ring, sign),
            device_id_type=MESH,
        )

    def text_message(par, ty, k):
        index = (par * 2 + ty) * (peers_grp - 1) + k - 1
        target = group_peer(k)
        return pltpu.make_async_remote_copy(
            src_ref=tsend.at[ty, target],
            dst_ref=trecv.at[par, ty, k - 1],
            send_sem=tssem.at[index],
            recv_sem=trsem.at[index],
            device_id=(target, s),
            device_id_type=MESH,
        )

    def columns(pair, ty):
        return pl.ds(pl.multiple_of((pair * 2 + ty) * LANES, LANES), LANES)

    def loads(pair):
        par = lax.rem(pair, 2)
        copies = []
        for ty in range(2):
            for a in range(4):
                copies.append(
                    pltpu.make_async_copy(
                        sources[a].at[:, columns(pair, ty)], inb.at[par, ty, a], insem.at[ty * 6 + a]
                    )
                )
        return copies

    def caption_loads(pair):
        copies = []
        for ty in range(2):
            for a, cap in enumerate((cap_keys, cap_values)):
                copies.append(
                    pltpu.make_async_copy(
                        cap.at[:, :, columns(pair, ty)], txt.at[ty, a], insem.at[ty * 6 + 4 + a]
                    )
                )
        return copies

    def stores(pair):
        copies = []
        for ty in range(2):
            for a in range(4):
                copies.append(
                    pltpu.make_async_copy(
                        stage.at[ty, a], outs[a].at[:, columns(pair, ty)], outsem.at[ty * 5 + a]
                    )
                )
            copies.append(
                pltpu.make_async_copy(
                    ttot.at[ty], out_text.at[:, :, columns(pair, ty)], outsem.at[ty * 5 + 4]
                )
            )
        return copies

    def fill(base, count, read):
        def step(k, carry):
            pool[base + k] = read(k)
            return carry

        lax.fori_loop(0, count, step, 0)

    def fill_own(io, par, ty):
        if io == 0:
            def step(j, carry):
                at = pl.ds(pl.multiple_of(j * TILE, TILE), TILE)
                for a in range(4):
                    pool[OWN + j, a] = inb[par, ty, a, at, :]
                return carry

            lax.fori_loop(0, 6, step, 0)
        else:
            fill(OWN, 9, lambda k: res[ty, k])

    def fill_arrived(io, par, ty):
        for sign in range(2):
            fill(DIRECT + sign * SLOTS, SLOTS, lambda k: recv_a[io, par, ty, sign, k])
            fill(FORWARD + sign * RELAY, RELAY, lambda k: recv_p[io, par, ty, sign, k])

    def fill_passing(io, par, ty):
        for sign in range(2):
            fill(PASSING + sign * RELAY, RELAY, lambda k: recv_m[io, par, ty, sign, k])

    def fill_final(io, par, ty):
        for sign in range(2):
            fill(FINAL + sign * SLOTS, RELAY, lambda k: recv_l[io, par, ty, sign, k])
            fill(
                FINAL + sign * SLOTS + RELAY,
                SLOTS - RELAY,
                lambda k: recv_m[io, par, ty, sign, RELAY + k],
            )

    def choose(ref, io, ty, entry, count):
        for sign in range(2):
            def step(k, carry):
                ref[io, ty, sign, k] = pool[plan[0, ty * P_SIZE + entry + sign * count + k]]
                return carry

            lax.fori_loop(0, count, step, 0)

    def begin(io, par, ty, kind):
        for sign in range(2):
            message(io, par, ty, sign, kind).start()

    def finish(io, par, ty, kind):
        for sign in range(2):
            message(io, par, ty, sign, kind).wait()

    def first_send(io, par, ty):
        fill_own(io, par, ty)
        choose(send_a, io, ty, P_BACK if io else P_SEND, SLOTS)
        begin(io, par, ty, SEND)

    def pass_on(io, par):
        for ty in range(2):
            finish(io, par, ty, SEND)
            begin(io, par, ty, PASS)

    def turn(io, par):
        for ty in range(2):
            finish(io, par, ty, PASS)
            fill_own(io, par, ty)
            fill_arrived(io, par, ty)
            choose(send_m, io, ty, P_BACK_MID if io else P_MID, SLOTS)
            begin(io, par, ty, MID)

    def last_send(io, par):
        for ty in range(2):
            finish(io, par, ty, MID)
            fill_own(io, par, ty)
            fill_arrived(io, par, ty)
            fill_passing(io, par, ty)
            choose(send_l, io, ty, P_BACK_LATE if io else P_LATE, RELAY)
            begin(io, par, ty, LATE)

    def compute(ty):
        tsend[ty] = jnp.zeros(tsend.shape[1:], tsend.dtype)

        def image(i, carry):
            tiles = tab[row, T_COUNT + i]
            caption = tab[row, T_CAPTION + i]
            length = tab[caption * (RING * RING), T_LENGTH]
            at = [plan[0, ty * P_SIZE + P_IMAGE + i * 3 + j] for j in range(3)]
            q = jnp.concatenate([pool[p, 0] for p in at], axis=0)
            k = jnp.concatenate([pool[p, 1] for p in at] + [txt[ty, 0, caption]], axis=0)
            v = jnp.concatenate([pool[p, 2] for p in at] + [txt[ty, 1, caption]], axis=0)
            do = jnp.concatenate([pool[p, 3] for p in at], axis=0)
            rows_q, rows_k = q.shape[0], k.shape[0]
            q_row = lax.broadcasted_iota(jnp.int32, (rows_q, LANES), 0)
            do = jnp.where(q_row < tiles * TILE, do, jnp.zeros_like(do))
            q = q * jnp.asarray(HEAD_DIM**-0.5, q.dtype)
            k_row = lax.broadcasted_iota(jnp.int32, (rows_k, LANES), 0)
            seen = (k_row < tiles * TILE) | ((k_row >= rows_q) & (k_row < rows_q + length))
            bias = jnp.where(seen, 0.0, -1e30)
            bias = jnp.concatenate([bias] * (rows_q // LANES), axis=1)
            lane_q = lax.broadcasted_iota(jnp.int32, (rows_q, LANES), 1) < HEAD_DIM
            lane_k = lax.broadcasted_iota(jnp.int32, (rows_k, LANES), 1) < HEAD_DIM
            k_t = k.T
            v_t = v.T
            o_parts, dq_parts, dk_parts, dv_parts = [], [], [], []
            contract_lanes = (((1,), (1,)), ((), ()))
            f32 = jnp.float32
            for h in range(2):
                keep = lane_q if h == 0 else jnp.logical_not(lane_q)
                q_h = jnp.where(keep, q, jnp.zeros_like(q))
                do_h = jnp.where(keep, do, jnp.zeros_like(do))
                scores = lax.dot_general(k, q_h, contract_lanes, preferred_element_type=f32) + bias
                weights = jnp.exp(scores - jnp.max(scores, axis=0, keepdims=True))
                probs = weights * (1.0 / jnp.sum(weights, axis=0, keepdims=True))
                dprobs = lax.dot_general(v, do_h, contract_lanes, preferred_element_type=f32)
                total = jnp.sum(probs * dprobs, axis=0, keepdims=True)
                dscores = (probs * (dprobs - total)).astype(jnp.bfloat16)
                low = probs.astype(jnp.bfloat16)
                span = slice(h * HEAD_DIM, (h + 1) * HEAD_DIM)
                o_parts.append(jnp.dot(v_t[span], low, preferred_element_type=f32))
                dq_parts.append(jnp.dot(k_t[span], dscores, preferred_element_type=f32))
                dk_parts.append(jnp.dot(dscores, q, preferred_element_type=f32))
                dv_parts.append(jnp.dot(low, do, preferred_element_type=f32))
            o = jnp.concatenate(o_parts, axis=0).T.astype(jnp.bfloat16)
            dq = (jnp.concatenate(dq_parts, axis=0).T * HEAD_DIM**-0.5).astype(jnp.bfloat16)
            dk = jnp.where(lane_k, dk_parts[0], dk_parts[1])
            dv = jnp.where(lane_k, dv_parts[0], dv_parts[1])
            for j in range(3):
                rows = slice(j * TILE, (j + 1) * TILE)
                res[ty, i * 3 + j, 0] = o[rows]
                res[ty, i * 3 + j, 1] = dq[rows]
                res[ty, i * 3 + j, 2] = dk[rows].astype(jnp.bfloat16)
                res[ty, i * 3 + j, 3] = dv[rows].astype(jnp.bfloat16)
            dk_text, dv_text = dk[rows_q:], dv[rows_q:]

            def spread(c, inner):
                hit = jnp.where(caption == c, 1.0, 0.0)
                tsend[ty, c, 0] += dk_text * hit
                tsend[ty, c, 1] += dv_text * hit
                return inner

            lax.fori_loop(0, peers_grp, spread, 0)
            return carry

        lax.fori_loop(0, 3, image, 0)

    def work(pair):
        par = lax.rem(pair, 2)
        for copy in caption_loads(pair):
            copy.wait()
        for ty in range(2):
            finish(0, par, ty, LATE)
            fill_own(0, par, ty)
            fill_arrived(0, par, ty)
            fill_final(0, par, ty)
            compute(ty)
            first_send(1, par, ty)
            for k in range(1, peers_grp):
                text_message(par, ty, k).start()

    def home(pair):
        par = lax.rem(pair, 2)

        @pl.when(pair > 0)
        def _():
            for copy in stores(pair - 1):
                copy.wait()

        for ty in range(2):
            finish(1, par, ty, LATE)
            fill_own(1, par, ty)
            fill_arrived(1, par, ty)
            fill_final(1, par, ty)

            def place(j, carry):
                at = pl.ds(pl.multiple_of(j * TILE, TILE), TILE)
                for a in range(4):
                    stage[ty, a, at, :] = pool[plan[0, ty * P_SIZE + P_HOME + j], a]
                return carry

            lax.fori_loop(0, 6, place, 0)
            for k in range(1, peers_grp):
                text_message(par, ty, k).wait()
            total = tsend[ty, g]
            for k in range(1, peers_grp):
                total = total + trecv[par, ty, k - 1]
            ttot[ty] = total
        for copy in stores(pair):
            copy.start()

    for copy in loads(0):
        copy.start()
    pl.semaphore_wait(barrier, 4 + peers_grp - 1)

    def superstep(step, carry):
        entering = step < pairs
        working = (step >= 1) & (step <= pairs)
        par_in = lax.rem(step, 2)
        par_out = lax.rem(step + 1, 2)

        @pl.when(step >= 2)
        def _():
            home(step - 2)

        @pl.when(entering)
        def _():
            for copy in loads(step):
                copy.wait()
            for ty in range(2):
                first_send(0, par_in, ty)

        @pl.when(working)
        def _():
            work(step - 1)

        @pl.when(step + 1 < pairs)
        def _():
            for copy in loads(step + 1):
                copy.start()

        @pl.when(entering)
        def _():
            for copy in caption_loads(step):
                copy.start()

        @pl.when(working)
        def _():
            pass_on(1, par_out)

        @pl.when(entering)
        def _():
            pass_on(0, par_in)

        @pl.when(working)
        def _():
            turn(1, par_out)

        @pl.when(entering)
        def _():
            turn(0, par_in)

        @pl.when(working)
        def _():
            last_send(1, par_out)

        @pl.when(entering)
        def _():
            last_send(0, par_in)

        return carry

    lax.fori_loop(0, pairs + 2, superstep, 0)
    for copy in stores(pairs - 1):
        copy.wait()


def body(
    image_queries,
    image_keys,
    image_values,
    cotangent,
    text_keys,
    text_values,
    text_lengths,
    send_owner,
    recv_source,
    tile_counts,
    caption_ids,
):
    rows, width = image_queries.shape
    peers_grp = lax.axis_size("grp")
    pairs = width // (2 * LANES)
    mine = jnp.concatenate(
        [send_owner[0], recv_source[0], tile_counts[0], caption_ids[0], text_lengths]
    ).astype(jnp.int32)
    mine = jnp.pad(mine, (0, LANES - mine.shape[0]))[None, :]
    table = lax.all_gather(mine, ("grp", "seq"), axis=0, tiled=True)
    all_keys = lax.all_gather(text_keys, "grp", axis=0, tiled=True)
    all_values = lax.all_gather(text_values, "grp", axis=0, tiled=True)
    vmem = pl.BlockSpec(memory_space=pltpu.VMEM)
    smem = pl.BlockSpec(memory_space=pltpu.SMEM)
    anywhere = pl.BlockSpec(memory_space=pl.ANY)
    plan = pl.pallas_call(
        plan_kernel,
        out_shape=jax.ShapeDtypeStruct((8, 2 * P_SIZE), jnp.int32),
        in_specs=[vmem, smem],
        out_specs=vmem,
        name="plan",
    )(table, mine)
    bf16, f32 = jnp.bfloat16, jnp.float32
    quad = (4, TILE, LANES)
    text_rows = text_keys.shape[1]
    image = jax.ShapeDtypeStruct((rows, width), bf16)
    scratch = [
        pltpu.VMEM((2, 2, 4, rows, LANES), bf16),
        pltpu.VMEM((2, 2, peers_grp, text_rows, LANES), bf16),
        pltpu.VMEM((2, 2, 2, SLOTS) + quad, bf16),
        pltpu.VMEM((2, 2, 2, 2, SLOTS) + quad, bf16),
        pltpu.VMEM((2, 2, 2, 2, RELAY) + quad, bf16),
        pltpu.VMEM((2, 2, 2, SLOTS) + quad, bf16),
        pltpu.VMEM((2, 2, 2, 2, SLOTS) + quad, bf16),
        pltpu.VMEM((2, 2, 2, RELAY) + quad, bf16),
        pltpu.VMEM((2, 2, 2, 2, RELAY) + quad, bf16),
        pltpu.VMEM((POOL,) + quad, bf16),
        pltpu.VMEM((2, 9) + quad, bf16),
        pltpu.VMEM((2, 4, rows, LANES), bf16),
        pltpu.VMEM((2, peers_grp, 2, text_rows, LANES), f32),
        pltpu.VMEM((2, 2, peers_grp - 1, 2, text_rows, LANES), f32),
        pltpu.VMEM((2, 2, text_rows, LANES), f32),
        pltpu.SemaphoreType.DMA((64,)),
        pltpu.SemaphoreType.DMA((64,)),
        pltpu.SemaphoreType.DMA((4 * (peers_grp - 1),)),
        pltpu.SemaphoreType.DMA((4 * (peers_grp - 1),)),
        pltpu.SemaphoreType.DMA((12,)),
        pltpu.SemaphoreType.DMA((10,)),
    ]
    attended, grad_queries, grad_keys, grad_values, text = pl.pallas_call(
        functools.partial(main_kernel, peers_grp, pairs),
        out_shape=(image, image, image, image, jax.ShapeDtypeStruct((2, text_rows, width), f32)),
        in_specs=[smem, smem] + [anywhere] * 6,
        out_specs=(anywhere,) * 5,
        scratch_shapes=scratch,
        compiler_params=pltpu.CompilerParams(
            collective_id=0, has_side_effects=True, vmem_limit_bytes=63 * 2**20
        ),
        name="attend",
    )(plan, table, image_queries, image_keys, image_values, cotangent, all_keys, all_values)
    text = lax.psum(text, "seq").astype(bf16)
    return attended, grad_queries, grad_keys, grad_values, text[:1], text[1:]


def solution(mesh):
    tokens = P(("grp", "seq"), None)
    captions = P("grp", None, None)
    return jax.shard_map(
        body,
        mesh=mesh,
        in_specs=(tokens,) * 4 + (captions, captions, P("grp")) + (tokens,) * 4,
        out_specs=(tokens,) * 4 + (captions, captions),
        check_vma=False,
    )
```

time: 678 us -> 398 us (0.59); the launches traced: 669 us -> 397 us
  Pallas kernels: 0 us -> 239 us
  matrix products: 211 us -> 0 us
  waiting for transfers between devices: 179 us -> 1.66 us
  local copies, waits for them, and re-layouts: 96.9 us -> 8.17 us
  blocking collectives: 90 us -> 134 us
  starting transfers between devices: 43.5 us -> 0.08 us
  other arithmetic: 31.7 us -> 0 us
    pallas_call x0 -> x2, Pallas kernels: none -> 239 us  [the longest x1 237 us: body(): pl.pallas_call(functools.partial(main_kernel, peers_grp, pairs), out_shap...]
    all_to_all x8 -> x0, waiting for transfers between devices: 179 us -> none  [the longest x1 43.3 us: body(): lax.all_to_all(outbound(image_queries), 'seq', split_axis=0, concat_axis=...]
    dot_general x50 -> x0, matrix products: 177 us -> none  [the longest x6 36.2 us: backward_pass(): jnp.einsum('qhd,khd->hqk', grad_heads, value_heads, preferred_element_typ...]
    all_gather x0 -> x1, blocking collectives: none -> 50.1 us  [body(): table = lax.all_gather(mine, ('grp', 'seq'), axis=0, tiled=True)]
    convert_element_type x28 -> x0, local copies, waits for them, and re-layouts: 44.9 us -> none  [the longest x4 12.6 us: homeward(): return jnp.einsum('tp,tnw->pnw', recv_pick, tensor.reshape(tile_count, ti...]
    all_to_all x8 -> x0, starting transfers between devices: 42.9 us -> none  [the longest x1 8.3 us: body(): lax.all_to_all(outbound(image_queries), 'seq', split_axis=0, concat_axis=...]
    sub x6 -> x0, matrix products: 34.1 us -> none  [probabilities(): weights = jnp.exp(scores - jnp.max(scores, axis=2, keepdims=True))]
    slice x37 -> x1, local copies, waits for them, and re-layouts: 24.6 us -> 0.77 us  [body(): return (attended, grad_queries, grad_keys, grad_values, text[:1], text[1:])]
  transfers between devices with their start and end apart: 12 -> 2, of which waited for: 7 -> 1; matrix products, arithmetic and copies ran while one was open for 26% -> 0% of each run, Pallas kernels for 0% -> 1%
where the time goes in v1:
time: 398 us; the launch traced here: 397 us
  Pallas kernels  239 us (60%)
  blocking collectives  134 us (34%)
  between operations  14.7 us (4%)
  local copies, waits for them, and re-layouts  8.17 us (2%)
    pallas_call x1, Pallas kernels, body(): pl.pallas_call(functools.partial(main_kernel, peers_grp, pairs), out_shap...  237 us
    psum x1, blocking collectives, body(): text = lax.psum(text, 'seq').astype(bf16)  83.6 us
    all_gather x1, blocking collectives, body(): table = lax.all_gather(mine, ('grp', 'seq'), axis=0, tiled=True)  50.1 us
  transfers between devices with their start and end apart: 2, of which 1 were waited for; matrix products, arithmetic and copies ran while one was open for 0% of the time, Pallas kernels for 1%

profile of v1, /device:TPU:0, one launch (start us, length us, event | category | flops | bytes accessed | tf_op | source)
XLA Modules:
  0.0 397.4 jit_solution(15451650252360059525)
XLA Ops:
  7.2 0.0 all-gather.5.cloned.1.call-start
  7.2 0.7 all-gather.5.cloned.1.call-update
  7.9 0.0 all-gather.7.cloned.1.call-start
  7.9 0.7 all-gather.7.cloned.1.call-update
  9.3 0.8 concatenate.3
  10.1 0.5 pad_bitcast_fusion.1
  10.6 50.1 %all-gather.1 = s32[128,1,128]{2,1,0:T(1,128)} all-gather(s32[1,1,128]{2,1,0:T(1,128)S(1)} %get-tuple-element.19), channel_id=2, replica_groups=mesh['grp'=8,'seq'=16] {'grp','seq'}, dimensions={0}, use_global_device_ids=true | all-gather | bytes 66048 | tf_op jit(solution)/shard_map/all_gather | solution.py:600
  60.7 2.1 plan.1
  62.8 0.0 all-gather.5.cloned.1.call-done.cap_keys
  62.8 0.3 all-gather.7.cloned.1.call-done.cap_values
  63.0 237.0 %attend.1 = (bf16[768,768]{1,0:T(8,128)(2,1)}, bf16[768,768]{1,0:T(8,128)(2,1)}, bf16[768,768]{1,0:T(8,128)(2,1)}, bf16[768,768]{1,0:T(8,128)(2,1)}, f32[2,128,768]{2,1,0:T(8,128)}) custom-call(s32[8,128]{1,0:T(8,128)} %plan.1, s32[128,128]{1,0:T(8,128)} %bitcast.10, bf16[768,768]{1,0:T(8,128)(2,1)} %queries.1, bf16[768,768]{1,0:T(8,128)(2,1)} %keys.1, ...), custom_call_target="tpu_custom_call" | custom-call | tf_op jit(solution)/shard_map/attend/pallas_call | solution.py:640
  300.0 0.0 copy-start.3
  300.0 83.6 %all-reduce.2 = bf16[2,128,768]{2,1,0:T(8,128)(2,1)S(1)} all-reduce(f32[2,128,768]{2,1,0:T(8,128)} %get-tuple-element.15), channel_id=1, replica_groups=mesh['grp'=8,'seq'=16] {'seq'}, use_global_device_ids=true, to_apply=%region_0.1 | all-reduce | flops 196608 | bytes 1179648 | tf_op jit(solution)/shard_map/psum | solution.py:651
  383.7 0.8 fusion
  384.4 0.0 copy-done.3
  384.4 1.0 copy.25
  385.5 0.7 copy-done.2
  386.1 0.0 copy-start.1
  386.1 1.0 copy.26
  387.2 0.7 copy-done.1
  387.8 0.0 copy-start
  387.8 1.0 copy.27
  388.9 0.7 copy-done
  389.5 1.0 copy.28
  (1 shorter events, 0.0 us)
Async XLA Ops:
  7.2 55.6 %all-gather.5.cloned.1.call-start = ((), (), s32[]{:S(2)}) async-start(), calls=%async_computation | async-start | bytes 1769472 | tf_op jit(solution)/shard_map/all_gather | solution.py:601
  7.9 55.1 %all-gather.7.cloned.1.call-start = ((), (), s32[]{:S(2)}) async-start(), calls=%async_computation.1 | async-start | bytes 1769472 | tf_op jit(solution)/shard_map/all_gather | solution.py:602
  300.0 84.4 %copy-start.3 = (bf16[768,768]{1,0:T(8,128)(2,1)S(1)}, bf16[768,768]{1,0:T(8,128)(2,1)}, u32[]{:S(2)}) copy-start(bf16[768,768]{1,0:T(8,128)(2,1)} %get-tuple-element.26) | copy-start | bytes 3538948
  384.4 1.7 copy-start.2
  386.1 1.7 copy-start.1
  387.8 1.7 copy-start
Sparse Core Ops, SparseCore 0:
  9.7 26.9 all-gather.4
  38.3 24.6 all-gather.6

commit v2 on v1

--- a/solution.py
+++ b/solution.py
@@ -31,6 +31,7 @@
 P_BACK_MID = 40
 P_BACK_LATE = 48
 P_HOME = 52
+P_LENGTH = 58
 P_SIZE = 64
 
 T_RECV, T_COUNT, T_CAPTION, T_LENGTH = 6, 12, 15, 18
@@ -38,11 +39,8 @@
 SEND, PASS, MID, LATE = range(4)
 
 
-def plan_kernel(tab_ref, row_ref, out_ref):
-    g = lax.axis_index("grp")
-    me = lax.axis_index("seq")
-    peers = 16
-    tab = tab_ref[pl.ds(pl.multiple_of(g * peers, peers), peers), :]
+def make_plan(tab, row_ref, lengths, me):
+    peers = tab.shape[0]
     src = lax.broadcasted_iota(jnp.int32, (peers, LANES), 0)
     own = lax.broadcasted_iota(jnp.int32, (peers, LANES), 1)
     sends = jnp.zeros((peers, LANES), jnp.int32)
@@ -179,18 +177,26 @@
                 put(P_IMAGE + i * 3 + j, mine_own & (src == row_ref[0, T_RECV + r]), there_end)
         for j in range(6):
             put(P_HOME + j, mine_src & (place == j), back_end)
+        if lengths is not None:
+            captions = lax.broadcasted_iota(jnp.int32, lengths.shape, 0)
+            column = lax.broadcasted_iota(jnp.int32, lengths.shape, 1) == T_LENGTH
+            for i in range(3):
+                put(P_LENGTH + i, column & (captions == row_ref[0, T_CAPTION + i]), lengths)
         rows.extend(part.get(entry, zero_row) for entry in range(P_SIZE))
     matrix = jnp.concatenate(rows, axis=0)
     ones = jnp.ones((8, LANES), jnp.float32)
     out = lax.dot_general(ones, matrix, (((1,), (1,)), ((), ())), preferred_element_type=jnp.float32)
-    out_ref[...] = out.astype(jnp.int32)
+    out = out.astype(jnp.int32)
+    entry = lax.broadcasted_iota(jnp.int32, out.shape, 1) % P_SIZE
+    return jnp.where(entry < P_LENGTH, jnp.clip(out, 0, POOL - 1), out)
 
 
 def main_kernel(
     peers_grp,
+    peers_seq,
     pairs,
-    plan,
-    tab,
+    mine,
+    mine_rows,
     queries,
     keys,
     values,
@@ -201,8 +207,15 @@
     out_queries,
     out_keys,
     out_values,
-    out_text,
+    out_cap_keys,
+    out_cap_values,
+    tab_seq,
+    tab_grp,
+    plan_rows,
+    plan_own,
+    plan,
     inb,
+    caps,
     txt,
     send_a,
     recv_a,
@@ -217,17 +230,28 @@
     tsend,
     trecv,
     ttot,
+    tpart,
+    tdone,
+    tall,
     ssem,
     rsem,
+    tabssem,
+    tabrsem,
+    capssem,
+    caprsem,
     tssem,
     trsem,
+    sumssem,
+    sumrsem,
+    endssem,
+    endrsem,
     insem,
     outsem,
+    plansem,
 ):
     g = lax.axis_index("grp")
     s = lax.axis_index("seq")
     z, y = lax.div(s, RING), lax.rem(s, RING)
-    row = g * (RING * RING) + s
     sources = (queries, keys, values, grads)
     outs = (out_rows, out_queries, out_keys, out_values)
 
@@ -240,10 +264,12 @@
     def group_peer(k):
         return lax.rem(g + k, peers_grp)
 
+    def seq_peer(k):
+        return lax.rem(s + k, peers_seq)
+
     barrier = pltpu.get_barrier_semaphore()
-    for ring in ("y", "z"):
-        for sign in (0, 1):
-            pl.semaphore_signal(barrier, inc=1, device_id=neighbour(ring, sign), device_id_type=MESH)
+    for k in range(1, peers_seq):
+        pl.semaphore_signal(barrier, inc=1, device_id=(g, seq_peer(k)), device_id_type=MESH)
     for k in range(1, peers_grp):
         pl.semaphore_signal(barrier, inc=1, device_id=(group_peer(k), s), device_id_type=MESH)
 
@@ -279,6 +305,81 @@
             device_id_type=MESH,
         )
 
+    def table_messages():
+        copies = []
+        for k in range(1, peers_seq + peers_grp - 1):
+            seq = k < peers_seq
+            copies.append(
+                pltpu.make_async_remote_copy(
+                    src_ref=mine_rows,
+                    dst_ref=tab_seq.at[s] if seq else tab_grp.at[g],
+                    send_sem=tabssem.at[k - 1],
+                    recv_sem=tabrsem.at[k - 1],
+                    device_id=(g, seq_peer(k)) if seq else (group_peer(k - peers_seq + 1), s),
+                    device_id_type=MESH,
+                )
+            )
+        return copies
+
+    def caption_messages(pair):
+        copies = []
+        for a, cap in enumerate((cap_keys, cap_values)):
+            src = cap.at[0, :, wide(pair)]
+            dst = caps.at[pair, g, a]
+            for k in range(1, peers_grp):
+                index = (pair * 2 + a) * (peers_grp - 1) + k - 1
+                copies.append(
+                    pltpu.make_async_remote_copy(
+                        src_ref=src,
+                        dst_ref=dst,
+                        send_sem=capssem.at[index],
+                        recv_sem=caprsem.at[index],
+                        device_id=(group_peer(k), s),
+                        device_id_type=MESH,
+                    )
+                )
+            copies.append(pltpu.make_async_copy(src, dst, insem.at[8 + pair * 2 + a]))
+        return copies
+
+    share = 16
+
+    def sum_messages(par):
+        copies = []
+        for k in range(1, peers_seq):
+            target = seq_peer(k)
+            index = par * (peers_seq - 1) + k - 1
+            copies.append(
+                pltpu.make_async_remote_copy(
+                    src_ref=ttot.at[par, pl.ds(pl.multiple_of(target * share, share), share)],
+                    dst_ref=tpart.at[par, k - 1],
+                    send_sem=sumssem.at[index],
+                    recv_sem=sumrsem.at[index],
+                    device_id=(g, target),
+                    device_id_type=MESH,
+                )
+            )
+        return copies
+
+    def end_messages(pair):
+        copies = []
+        at = pl.ds(pl.multiple_of(s * share, share), share)
+        for k in range(1, peers_seq):
+            index = pair * (peers_seq - 1) + k - 1
+            copies.append(
+                pltpu.make_async_remote_copy(
+                    src_ref=tdone.at[pair],
+                    dst_ref=tall.at[pair, at],
+                    send_sem=endssem.at[index],
+                    recv_sem=endrsem.at[index],
+                    device_id=(g, seq_peer(k)),
+                    device_id_type=MESH,
+                )
+            )
+        return copies
+
+    def wide(pair):
+        return pl.ds(pl.multiple_of(pair * (2 * LANES), 2 * LANES), 2 * LANES)
+
     def columns(pair, ty):
         return pl.ds(pl.multiple_of((pair * 2 + ty) * LANES, LANES), LANES)
 
@@ -289,18 +390,7 @@
             for a in range(4):
                 copies.append(
                     pltpu.make_async_copy(
-                        sources[a].at[:, columns(pair, ty)], inb.at[par, ty, a], insem.at[ty * 6 + a]
-                    )
-                )
-        return copies
-
-    def caption_loads(pair):
-        copies = []
-        for ty in range(2):
-            for a, cap in enumerate((cap_keys, cap_values)):
-                copies.append(
-                    pltpu.make_async_copy(
-                        cap.at[:, :, columns(pair, ty)], txt.at[ty, a], insem.at[ty * 6 + 4 + a]
+                        sources[a].at[:, columns(pair, ty)], inb.at[par, ty, a], insem.at[ty * 4 + a]
                     )
                 )
         return copies
@@ -311,12 +401,14 @@
             for a in range(4):
                 copies.append(
                     pltpu.make_async_copy(
-                        stage.at[ty, a], outs[a].at[:, columns(pair, ty)], outsem.at[ty * 5 + a]
+                        stage.at[ty, a], outs[a].at[:, columns(pair, ty)], outsem.at[ty * 4 + a]
                     )
                 )
+        rows = tall.shape[1] // 2
+        for a, out in enumerate((out_cap_keys, out_cap_values)):
             copies.append(
                 pltpu.make_async_copy(
-                    ttot.at[ty], out_text.at[:, :, columns(pair, ty)], outsem.at[ty * 5 + 4]
+                    tall.at[pair, pl.ds(a * rows, rows)], out.at[0, :, wide(pair)], outsem.at[8 + a]
                 )
             )
         return copies
@@ -358,10 +450,10 @@
                 lambda k: recv_m[io, par, ty, sign, RELAY + k],
             )
 
-    def choose(ref, io, ty, entry, count):
+    def choose(ref, io, ty, entry, count, table=plan):
         for sign in range(2):
             def step(k, carry):
-                ref[io, ty, sign, k] = pool[plan[0, ty * P_SIZE + entry + sign * count + k]]
+                ref[io, ty, sign, k] = pool[table[0, ty * P_SIZE + entry + sign * count + k]]
                 return carry
 
             lax.fori_loop(0, count, step, 0)
@@ -374,9 +466,9 @@
         for sign in range(2):
             message(io, par, ty, sign, kind).wait()
 
-    def first_send(io, par, ty):
+    def first_send(io, par, ty, table=plan):
         fill_own(io, par, ty)
-        choose(send_a, io, ty, P_BACK if io else P_SEND, SLOTS)
+        choose(send_a, io, ty, P_BACK if io else P_SEND, SLOTS, table)
         begin(io, par, ty, SEND)
 
     def pass_on(io, par):
@@ -405,9 +497,9 @@
         tsend[ty] = jnp.zeros(tsend.shape[1:], tsend.dtype)
 
         def image(i, carry):
-            tiles = tab[row, T_COUNT + i]
-            caption = tab[row, T_CAPTION + i]
-            length = tab[caption * (RING * RING), T_LENGTH]
+            tiles = mine[0, T_COUNT + i]
+            caption = mine[0, T_CAPTION + i]
+            length = plan[0, P_LENGTH + i]
             at = [plan[0, ty * P_SIZE + P_IMAGE + i * 3 + j] for j in range(3)]
             q = jnp.concatenate([pool[p, 0] for p in at], axis=0)
             k = jnp.concatenate([pool[p, 1] for p in at] + [txt[ty, 0, caption]], axis=0)
@@ -469,8 +561,16 @@
 
     def work(pair):
         par = lax.rem(pair, 2)
-        for copy in caption_loads(pair):
+        for copy in caption_messages(pair):
             copy.wait()
+
+        def current(c, carry):
+            for a in range(2):
+                for ty in range(2):
+                    txt[ty, a, c] = caps[pair, c, a, :, ty * LANES : (ty + 1) * LANES]
+            return carry
+
+        lax.fori_loop(0, peers_grp, current, 0)
         for ty in range(2):
             finish(0, par, ty, LATE)
             fill_own(0, par, ty)
@@ -502,18 +602,67 @@
                 return carry
 
             lax.fori_loop(0, 6, place, 0)
+        for copy in end_messages(pair):
+            copy.wait()
+        for copy in stores(pair):
+            copy.start()
+
+    def add_captions(pair):
+        par = lax.rem(pair, 2)
+        for ty in range(2):
             for k in range(1, peers_grp):
                 text_message(par, ty, k).wait()
-            total = tsend[ty, g]
-            for k in range(1, peers_grp):
-                total = total + trecv[par, ty, k - 1]
-            ttot[ty] = total
-        for copy in stores(pair):
+            at = slice(ty * LANES, (ty + 1) * LANES)
+            for a in range(2):
+                total = tsend[ty, g, a]
+                for k in range(1, peers_grp):
+                    total = total + trecv[par, ty, k - 1, a]
+                ttot[par, a * TILE : (a + 1) * TILE, at] = total
+        for copy in sum_messages(par):
+            copy.start()
+
+    def end_captions(pair):
+        par = lax.rem(pair, 2)
+        for copy in sum_messages(par):
+            copy.wait()
+        at = pl.ds(pl.multiple_of(s * share, share), share)
+        total = ttot[par, at, :]
+        for k in range(1, peers_seq):
+            total = total + tpart[par, k - 1]
+        done = total.astype(tdone.dtype)
+        tdone[pair] = done
+        tall[pair, at, :] = done
+        for copy in end_messages(pair):
             copy.start()
 
     for copy in loads(0):
         copy.start()
-    pl.semaphore_wait(barrier, 4 + peers_grp - 1)
+    own_rows = mine_rows[...]
+    tab_seq[s] = own_rows
+    tab_grp[g] = own_rows
+
+    def publish(values, place):
+        plan_rows[...] = values
+        copy = pltpu.make_async_copy(plan_rows, place, plansem)
+        copy.start()
+        copy.wait()
+
+    source = lax.broadcasted_iota(jnp.int32, (peers_seq, LANES), 0)
+    alone = jnp.where(source == s, jnp.concatenate([own_rows] * (peers_seq // 8), axis=0), -1)
+    publish(make_plan(alone, mine, None, s), plan_own)
+    pl.semaphore_wait(barrier, peers_seq + peers_grp - 2)
+    for copy in table_messages():
+        copy.start()
+    for copy in loads(0):
+        copy.wait()
+    for ty in range(2):
+        first_send(0, 0, ty, plan_own)
+    for pair in range(pairs):
+        for copy in caption_messages(pair):
+            copy.start()
+    for copy in table_messages():
+        copy.wait()
+    publish(make_plan(tab_seq[:, 0, :], mine, tab_grp[:, 0, :], s), plan)
 
     def superstep(step, carry):
         entering = step < pairs
@@ -525,7 +674,7 @@
         def _():
             home(step - 2)
 
-        @pl.when(entering)
+        @pl.when(entering & (step > 0))
         def _():
             for copy in loads(step):
                 copy.wait()
@@ -541,30 +690,27 @@
             for copy in loads(step + 1):
                 copy.start()
 
+        @pl.when(working)
+        def _():
+            pass_on(1, par_out)
+            add_captions(step - 1)
+
         @pl.when(entering)
         def _():
-            for copy in caption_loads(step):
-                copy.start()
+            pass_on(0, par_in)
 
         @pl.when(working)
         def _():
-            pass_on(1, par_out)
+            turn(1, par_out)
 
         @pl.when(entering)
         def _():
-            pass_on(0, par_in)
+            turn(0, par_in)
 
         @pl.when(working)
         def _():
-            turn(1, par_out)
-
-        @pl.when(entering)
-        def _():
-            turn(0, par_in)
-
-        @pl.when(working)
-        def _():
             last_send(1, par_out)
+            end_captions(step - 1)
 
         @pl.when(entering)
         def _():
@@ -591,31 +737,29 @@
     caption_ids,
 ):
     rows, width = image_queries.shape
-    peers_grp = lax.axis_size("grp")
+    peers_grp, peers_seq = lax.axis_size("grp"), lax.axis_size("seq")
     pairs = width // (2 * LANES)
     mine = jnp.concatenate(
         [send_owner[0], recv_source[0], tile_counts[0], caption_ids[0], text_lengths]
     ).astype(jnp.int32)
-    mine = jnp.pad(mine, (0, LANES - mine.shape[0]))[None, :]
-    table = lax.all_gather(mine, ("grp", "seq"), axis=0, tiled=True)
-    all_keys = lax.all_gather(text_keys, "grp", axis=0, tiled=True)
-    all_values = lax.all_gather(text_values, "grp", axis=0, tiled=True)
+    mine = jnp.broadcast_to(jnp.pad(mine, (0, LANES - mine.shape[0]))[None, :], (8, LANES))
     vmem = pl.BlockSpec(memory_space=pltpu.VMEM)
     smem = pl.BlockSpec(memory_space=pltpu.SMEM)
     anywhere = pl.BlockSpec(memory_space=pl.ANY)
-    plan = pl.pallas_call(
-        plan_kernel,
-        out_shape=jax.ShapeDtypeStruct((8, 2 * P_SIZE), jnp.int32),
-        in_specs=[vmem, smem],
-        out_specs=vmem,
-        name="plan",
-    )(table, mine)
     bf16, f32 = jnp.bfloat16, jnp.float32
     quad = (4, TILE, LANES)
     text_rows = text_keys.shape[1]
     image = jax.ShapeDtypeStruct((rows, width), bf16)
+    caption = jax.ShapeDtypeStruct(text_keys.shape, bf16)
+    dma = pltpu.SemaphoreType.DMA
     scratch = [
+        pltpu.VMEM((peers_seq, 8, LANES), jnp.int32),
+        pltpu.VMEM((peers_grp, 8, LANES), jnp.int32),
+        pltpu.VMEM((8, 2 * P_SIZE), jnp.int32),
+        pltpu.SMEM((8, 2 * P_SIZE), jnp.int32),
+        pltpu.SMEM((8, 2 * P_SIZE), jnp.int32),
         pltpu.VMEM((2, 2, 4, rows, LANES), bf16),
+        pltpu.VMEM((pairs, peers_grp, 2, text_rows, 2 * LANES), bf16),
         pltpu.VMEM((2, 2, peers_grp, text_rows, LANES), bf16),
         pltpu.VMEM((2, 2, 2, SLOTS) + quad, bf16),
         pltpu.VMEM((2, 2, 2, 2, SLOTS) + quad, bf16),
@@ -629,27 +773,37 @@
         pltpu.VMEM((2, 4, rows, LANES), bf16),
         pltpu.VMEM((2, peers_grp, 2, text_rows, LANES), f32),
         pltpu.VMEM((2, 2, peers_grp - 1, 2, text_rows, LANES), f32),
-        pltpu.VMEM((2, 2, text_rows, LANES), f32),
-        pltpu.SemaphoreType.DMA((64,)),
-        pltpu.SemaphoreType.DMA((64,)),
-        pltpu.SemaphoreType.DMA((4 * (peers_grp - 1),)),
-        pltpu.SemaphoreType.DMA((4 * (peers_grp - 1),)),
-        pltpu.SemaphoreType.DMA((12,)),
-        pltpu.SemaphoreType.DMA((10,)),
+        pltpu.VMEM((2, 2 * text_rows, 2 * LANES), f32),
+        pltpu.VMEM((2, peers_seq - 1, 2 * text_rows // peers_seq, 2 * LANES), f32),
+        pltpu.VMEM((pairs, 2 * text_rows // peers_seq, 2 * LANES), bf16),
+        pltpu.VMEM((pairs, 2 * text_rows, 2 * LANES), bf16),
+        dma((64,)),
+        dma((64,)),
+        dma((peers_seq + peers_grp - 2,)),
+        dma((peers_seq + peers_grp - 2,)),
+        dma((pairs * 2 * (peers_grp - 1),)),
+        dma((pairs * 2 * (peers_grp - 1),)),
+        dma((4 * (peers_grp - 1),)),
+        dma((4 * (peers_grp - 1),)),
+        dma((2 * (peers_seq - 1),)),
+        dma((2 * (peers_seq - 1),)),
+        dma((pairs * (peers_seq - 1),)),
+        dma((pairs * (peers_seq - 1),)),
+        dma((8 + 2 * pairs,)),
+        dma((10,)),
+        dma,
     ]
-    attended, grad_queries, grad_keys, grad_values, text = pl.pallas_call(
-        functools.partial(main_kernel, peers_grp, pairs),
-        out_shape=(image, image, image, image, jax.ShapeDtypeStruct((2, text_rows, width), f32)),
-        in_specs=[smem, smem] + [anywhere] * 6,
-        out_specs=(anywhere,) * 5,
+    return pl.pallas_call(
+        functools.partial(main_kernel, peers_grp, peers_seq, pairs),
+        out_shape=(image, image, image, image, caption, caption),
+        in_specs=[smem, vmem] + [anywhere] * 6,
+        out_specs=(anywhere,) * 6,
         scratch_shapes=scratch,
         compiler_params=pltpu.CompilerParams(
             collective_id=0, has_side_effects=True, vmem_limit_bytes=63 * 2**20
         ),
         name="attend",
-    )(plan, table, image_queries, image_keys, image_values, cotangent, all_keys, all_values)
-    text = lax.psum(text, "seq").astype(bf16)
-    return attended, grad_queries, grad_keys, grad_values, text[:1], text[1:]
+    )(mine, mine, image_queries, image_keys, image_values, cotangent, text_keys, text_values)
 
 
 def solution(mesh):

time: 398 us -> 278 us (0.70)
  blocking collectives: 134 us -> 0 us
  Pallas kernels: 239 us -> 266 us
  between operations: 14.7 us -> 1.3 us
    psum x1 -> x0, blocking collectives: 83.6 us -> none  [body(): text = lax.psum(text, 'seq').astype(bf16)]
    all_gather x1 -> x0, blocking collectives: 50.1 us -> none  [body(): table = lax.all_gather(mine, ('grp', 'seq'), axis=0, tiled=True)]
    pallas_call x2 -> x1, Pallas kernels: 239 us -> 266 us  [body(): pl.pallas_call(functools.partial(main_kernel, peers_grp, peers_seq, pairs...]
    unnamed x12 -> x16, local copies, waits for them, and re-layouts: 6.1 us -> 8.32 us
  transfers between devices with their start and end apart: 2 -> 0, of which waited for: 1 -> 0; matrix products, arithmetic and copies ran while one was open for 0% -> 0% of each run, Pallas kernels for 1% -> 0%
where the time goes in v2:
time: 278 us; the launch traced here: 277 us
  Pallas kernels  266 us (96%)
  local copies, waits for them, and re-layouts  9.7 us (3%)
    pallas_call x1, Pallas kernels, body(): pl.pallas_call(functools.partial(main_kernel, peers_grp, peers_seq, pairs...  266 us
    unnamed x16, local copies, waits for them, and re-layouts  8.32 us

profile of v2, /device:TPU:0, one launch (start us, length us, event | category | flops | bytes accessed | tf_op | source)
XLA Modules:
  0.0 277.3 jit_solution(14068697448903178774)
XLA Ops:
  1.3 0.8 concatenate.3
  2.1 0.6 broadcast_in_dim.2.mine.mine_rows
  2.7 266.3 %attend.1 = (bf16[768,768]{1,0:T(8,128)(2,1)}, bf16[768,768]{1,0:T(8,128)(2,1)}, bf16[768,768]{1,0:T(8,128)(2,1)}, bf16[768,768]{1,0:T(8,128)(2,1)}, bf16[1,128,...) custom-call(s32[8,128]{1,0:T(8,128)} %broadcast_in_dim.2.mine.mine_rows, s32[8,128]{1,0:T(8,128)} %broadcast_in_dim.2.mine.mine_rows, ...), custom_call_target="tpu_custom_call" | custom-call | tf_op jit(solution)/shard_map/attend/pallas_call | solution.py:796
  268.9 0.0 copy-start.2
  268.9 2.5 copy.24
  271.4 0.0 copy-done.2
  271.4 0.0 copy-start.1
  271.4 1.0 copy.25
  272.4 0.7 copy-done.1
  273.1 0.0 copy-start
  273.1 1.0 copy.26
  274.1 0.7 copy-done
  274.8 0.0 copy-start.4
  274.8 0.0 copy-start.3
  274.8 1.0 copy.27
  275.8 0.1 copy-done.4
  275.9 0.7 copy.28
  276.6 0.0 copy-done.3
  276.6 0.7 copy.29
  (1 shorter events, 0.0 us)
Async XLA Ops:
  268.9 2.5 copy-start.2
  271.4 1.7 copy-start.1
  273.1 1.7 copy-start
  274.8 1.1 copy-start.4
  274.8 1.8 copy-start.3

commit v3 on v2

--- a/solution.py
+++ b/solution.py
@@ -17,11 +17,11 @@
 RELAY = 2
 
 OWN = 0
-DIRECT = 9
-FORWARD = 17
-FINAL = 21
-PASSING = 29
-POOL = 33
+DIRECT = 6
+FORWARD = 14
+FINAL = 18
+PASSING = 26
+POOL = 30
 
 P_SEND = 0
 P_MID = 8
@@ -36,7 +36,8 @@
 
 T_RECV, T_COUNT, T_CAPTION, T_LENGTH = 6, 12, 15, 18
 
-SEND, PASS, MID, LATE = range(4)
+SEND, SEND_NEAR, PASS, MID, MID_NEAR, LATE = range(6)
+KINDS = 6
 
 
 def make_plan(tab, row_ref, lengths, me):
@@ -52,13 +53,8 @@
     first = row_ref[0, T_COUNT]
     second = first + row_ref[0, T_COUNT + 1]
     result = jnp.zeros((peers, LANES), jnp.int32)
-    padded = []
     for r in range(6):
-        image = jnp.where(r >= first, 1, 0) + jnp.where(r >= second, 1, 0)
-        begin = jnp.where(r >= second, second, jnp.where(r >= first, first, 0))
-        where_r = image * 3 + r - begin
-        padded.append(where_r)
-        result += jnp.where(src == row_ref[0, T_RECV + r], where_r, 0)
+        result += jnp.where(src == row_ref[0, T_RECV + r], r, 0)
 
     lower = (
         lax.broadcasted_iota(jnp.int32, (peers, peers), 1)
@@ -227,8 +223,19 @@
     pool,
     res,
     stage,
+    kk,
+    vv,
+    kt,
+    vt,
+    qm,
+    dm,
+    ps,
+    ds,
+    tgrad,
+    tself,
     tsend,
     trecv,
+    tsum,
     ttot,
     tpart,
     tdone,
@@ -273,17 +280,27 @@
     for k in range(1, peers_grp):
         pl.semaphore_signal(barrier, inc=1, device_id=(group_peer(k), s), device_id_type=MESH)
 
-    def message(io, par, ty, sign, kind):
+    def first_ring(io, pair):
+        return 2 + pair if io else lax.rem(pair, 2)
+
+    def second_ring(io, pair):
+        return io * 2 + lax.rem(pair, 2)
+
+    def message(io, pair, ty, sign, kind):
         ring = "y" if (ty + io + (1 if kind >= MID else 0)) % 2 == 0 else "z"
-        if kind == SEND:
-            src, dst = send_a.at[io, ty, sign], recv_a.at[io, par, ty, sign]
+        far, near = pl.ds(0, RELAY), pl.ds(RELAY, SLOTS - RELAY)
+        one, two = first_ring(io, pair), second_ring(io, pair)
+        if kind in (SEND, SEND_NEAR):
+            at = far if kind == SEND else near
+            src, dst = send_a.at[io, ty, sign, at], recv_a.at[one, ty, sign, at]
         elif kind == PASS:
-            src, dst = recv_a.at[io, par, ty, sign, pl.ds(0, RELAY)], recv_p.at[io, par, ty, sign]
-        elif kind == MID:
-            src, dst = send_m.at[io, ty, sign], recv_m.at[io, par, ty, sign]
+            src, dst = recv_a.at[one, ty, sign, far], recv_p.at[one, ty, sign]
+        elif kind in (MID, MID_NEAR):
+            at = far if kind == MID else near
+            src, dst = send_m.at[io, ty, sign, at], recv_m.at[two, ty, sign, at]
         else:
-            src, dst = send_l.at[io, ty, sign], recv_l.at[io, par, ty, sign]
-        index = (((io * 2 + par) * 2 + ty) * 2 + sign) * 4 + kind
+            src, dst = send_l.at[io, ty, sign], recv_l.at[two, ty, sign]
+        index = ((one * 2 + ty) * 2 + sign) * KINDS + kind
         return pltpu.make_async_remote_copy(
             src_ref=src,
             dst_ref=dst,
@@ -404,13 +421,20 @@
                         stage.at[ty, a], outs[a].at[:, columns(pair, ty)], outsem.at[ty * 4 + a]
                     )
                 )
+        return copies
+
+    def caption_stores():
         rows = tall.shape[1] // 2
-        for a, out in enumerate((out_cap_keys, out_cap_values)):
-            copies.append(
-                pltpu.make_async_copy(
-                    tall.at[pair, pl.ds(a * rows, rows)], out.at[0, :, wide(pair)], outsem.at[8 + a]
+        copies = []
+        for pair in range(pairs):
+            for a, out in enumerate((out_cap_keys, out_cap_values)):
+                copies.append(
+                    pltpu.make_async_copy(
+                        tall.at[pair, pl.ds(a * rows, rows)],
+                        out.at[0, :, wide(pair)],
+                        outsem.at[8 + pair * 2 + a],
+                    )
                 )
-            )
         return copies
 
     def fill(base, count, read):
@@ -420,180 +444,240 @@
 
         lax.fori_loop(0, count, step, 0)
 
-    def fill_own(io, par, ty):
-        if io == 0:
-            def step(j, carry):
-                at = pl.ds(pl.multiple_of(j * TILE, TILE), TILE)
-                for a in range(4):
-                    pool[OWN + j, a] = inb[par, ty, a, at, :]
-                return carry
-
-            lax.fori_loop(0, 6, step, 0)
-        else:
-            fill(OWN, 9, lambda k: res[ty, k])
-
-    def fill_arrived(io, par, ty):
+    def fill_own(io, pair, ty):
+        par = lax.rem(pair, 2)
+        if io:
+            fill(OWN, 6, lambda k: res[par, ty, k])
+            return
+
+        def step(j, carry):
+            at = pl.ds(pl.multiple_of(j * TILE, TILE), TILE)
+            for a in range(4):
+                pool[OWN + j, a] = inb[par, ty, a, at, :]
+            return carry
+
+        lax.fori_loop(0, 6, step, 0)
+
+    def fill_arrived(io, pair, ty):
+        one = first_ring(io, pair)
         for sign in range(2):
-            fill(DIRECT + sign * SLOTS, SLOTS, lambda k: recv_a[io, par, ty, sign, k])
-            fill(FORWARD + sign * RELAY, RELAY, lambda k: recv_p[io, par, ty, sign, k])
-
-    def fill_passing(io, par, ty):
+            fill(DIRECT + sign * SLOTS, SLOTS, lambda k: recv_a[one, ty, sign, k])
+            fill(FORWARD + sign * RELAY, RELAY, lambda k: recv_p[one, ty, sign, k])
+
+    def fill_passing(io, pair, ty):
+        two = second_ring(io, pair)
         for sign in range(2):
-            fill(PASSING + sign * RELAY, RELAY, lambda k: recv_m[io, par, ty, sign, k])
-
-    def fill_final(io, par, ty):
+            fill(PASSING + sign * RELAY, RELAY, lambda k: recv_m[two, ty, sign, k])
+
+    def fill_final(io, pair, ty):
+        two = second_ring(io, pair)
         for sign in range(2):
-            fill(FINAL + sign * SLOTS, RELAY, lambda k: recv_l[io, par, ty, sign, k])
+            fill(FINAL + sign * SLOTS, RELAY, lambda k: recv_l[two, ty, sign, k])
             fill(
                 FINAL + sign * SLOTS + RELAY,
                 SLOTS - RELAY,
-                lambda k: recv_m[io, par, ty, sign, RELAY + k],
+                lambda k: recv_m[two, ty, sign, RELAY + k],
             )
 
-    def choose(ref, io, ty, entry, count, table=plan):
+    def choose(ref, io, ty, entry, count, first, last, table=plan):
         for sign in range(2):
+
             def step(k, carry):
                 ref[io, ty, sign, k] = pool[table[0, ty * P_SIZE + entry + sign * count + k]]
                 return carry
 
-            lax.fori_loop(0, count, step, 0)
-
-    def begin(io, par, ty, kind):
+            lax.fori_loop(first, last, step, 0)
+
+    def begin(io, pair, ty, kind):
         for sign in range(2):
-            message(io, par, ty, sign, kind).start()
-
-    def finish(io, par, ty, kind):
+            message(io, pair, ty, sign, kind).start()
+
+    def finish(io, pair, ty, kind):
         for sign in range(2):
-            message(io, par, ty, sign, kind).wait()
-
-    def first_send(io, par, ty, table=plan):
-        fill_own(io, par, ty)
-        choose(send_a, io, ty, P_BACK if io else P_SEND, SLOTS, table)
-        begin(io, par, ty, SEND)
-
-    def pass_on(io, par):
+            message(io, pair, ty, sign, kind).wait()
+
+    def first_send(io, pair, ty, table=plan):
+        fill_own(io, pair, ty)
+        entry = P_BACK if io else P_SEND
+        choose(send_a, io, ty, entry, SLOTS, 0, RELAY, table)
+        begin(io, pair, ty, SEND)
+        choose(send_a, io, ty, entry, SLOTS, RELAY, SLOTS, table)
+        begin(io, pair, ty, SEND_NEAR)
+
+    def pass_on(io, pair):
         for ty in range(2):
-            finish(io, par, ty, SEND)
-            begin(io, par, ty, PASS)
-
-    def turn(io, par):
+            finish(io, pair, ty, SEND)
+            begin(io, pair, ty, PASS)
+
+    def turn(io, pair):
         for ty in range(2):
-            finish(io, par, ty, PASS)
-            fill_own(io, par, ty)
-            fill_arrived(io, par, ty)
-            choose(send_m, io, ty, P_BACK_MID if io else P_MID, SLOTS)
-            begin(io, par, ty, MID)
-
-    def last_send(io, par):
+            finish(io, pair, ty, SEND_NEAR)
+            finish(io, pair, ty, PASS)
+            fill_own(io, pair, ty)
+            fill_arrived(io, pair, ty)
+            entry = P_BACK_MID if io else P_MID
+            choose(send_m, io, ty, entry, SLOTS, 0, RELAY)
+            begin(io, pair, ty, MID)
+            choose(send_m, io, ty, entry, SLOTS, RELAY, SLOTS)
+            begin(io, pair, ty, MID_NEAR)
+
+    def last_send(io, pair):
         for ty in range(2):
-            finish(io, par, ty, MID)
-            fill_own(io, par, ty)
-            fill_arrived(io, par, ty)
-            fill_passing(io, par, ty)
-            choose(send_l, io, ty, P_BACK_LATE if io else P_LATE, RELAY)
-            begin(io, par, ty, LATE)
-
-    def compute(ty):
-        tsend[ty] = jnp.zeros(tsend.shape[1:], tsend.dtype)
-
-        def image(i, carry):
+            finish(io, pair, ty, MID)
+            fill_own(io, pair, ty)
+            fill_arrived(io, pair, ty)
+            fill_passing(io, pair, ty)
+            choose(send_l, io, ty, P_BACK_LATE if io else P_LATE, RELAY, 0, RELAY)
+            begin(io, pair, ty, LATE)
+
+    def final(io, pair, ty):
+        finish(io, pair, ty, MID_NEAR)
+        finish(io, pair, ty, LATE)
+        fill_own(io, pair, ty)
+        fill_arrived(io, pair, ty)
+        fill_final(io, pair, ty)
+
+    def compute(pair, ty):
+        par = lax.rem(pair, 2)
+        bf16, f32 = jnp.bfloat16, jnp.float32
+        scale = HEAD_DIM**-0.5
+        lane = lax.broadcasted_iota(jnp.int32, (TILE, LANES), 1) < HEAD_DIM
+        text_row = lax.broadcasted_iota(jnp.int32, (TILE, LANES), 0)
+        contract_lanes = (((1,), (1,)), ((), ()))
+        first = mine[0, T_COUNT]
+        second = first + mine[0, T_COUNT + 1]
+        text = 3 * TILE
+
+        def begin_of(i):
+            return jnp.where(i == 0, 0, jnp.where(i == 1, first, second))
+
+        def half(tile, h):
+            return jnp.where(lane if h == 0 else jnp.logical_not(lane), tile, jnp.zeros_like(tile))
+
+        def prepare(i, carry):
             tiles = mine[0, T_COUNT + i]
             caption = mine[0, T_CAPTION + i]
+            for j in range(4):
+                at = slice(j * TILE, (j + 1) * TILE)
+                if j < 3:
+                    place = plan[0, ty * P_SIZE + P_IMAGE + i * 3 + j]
+                    k, v = pool[place, 1], pool[place, 2]
+                    live = jnp.where(j < tiles, 1.0, 0.0)
+                    qm[i, at, :] = (pool[place, 0].astype(f32) * (live * scale)).astype(bf16)
+                    dm[i, at, :] = (pool[place, 3].astype(f32) * live).astype(bf16)
+                else:
+                    k, v = txt[0, caption], txt[1, caption]
+                kk[i, at, :] = k
+                vv[i, at, :] = v
+                kt[i, :, at] = k.T
+                vt[i, :, at] = v.T
+            return carry
+
+        lax.fori_loop(0, 3, prepare, 0)
+
+        def query(r, carry):
+            i = jnp.where(r >= first, 1, 0) + jnp.where(r >= second, 1, 0)
+            j = jnp.minimum(r - begin_of(i), 2)
+            tiles = mine[0, T_COUNT + i]
             length = plan[0, P_LENGTH + i]
-            at = [plan[0, ty * P_SIZE + P_IMAGE + i * 3 + j] for j in range(3)]
-            q = jnp.concatenate([pool[p, 0] for p in at], axis=0)
-            k = jnp.concatenate([pool[p, 1] for p in at] + [txt[ty, 0, caption]], axis=0)
-            v = jnp.concatenate([pool[p, 2] for p in at] + [txt[ty, 1, caption]], axis=0)
-            do = jnp.concatenate([pool[p, 3] for p in at], axis=0)
-            rows_q, rows_k = q.shape[0], k.shape[0]
-            q_row = lax.broadcasted_iota(jnp.int32, (rows_q, LANES), 0)
-            do = jnp.where(q_row < tiles * TILE, do, jnp.zeros_like(do))
-            q = q * jnp.asarray(HEAD_DIM**-0.5, q.dtype)
-            k_row = lax.broadcasted_iota(jnp.int32, (rows_k, LANES), 0)
-            seen = (k_row < tiles * TILE) | ((k_row >= rows_q) & (k_row < rows_q + length))
-            bias = jnp.where(seen, 0.0, -1e30)
-            bias = jnp.concatenate([bias] * (rows_q // LANES), axis=1)
-            lane_q = lax.broadcasted_iota(jnp.int32, (rows_q, LANES), 1) < HEAD_DIM
-            lane_k = lax.broadcasted_iota(jnp.int32, (rows_k, LANES), 1) < HEAD_DIM
-            k_t = k.T
-            v_t = v.T
-            o_parts, dq_parts, dk_parts, dv_parts = [], [], [], []
-            contract_lanes = (((1,), (1,)), ((), ()))
-            f32 = jnp.float32
+            place = plan[0, ty * P_SIZE + P_IMAGE + i * 3 + j]
+            q = pool[place, 0] * jnp.asarray(scale, bf16)
+            do = pool[place, 3]
+            k, v = kk[i], vv[i]
+            hide = [0.0] + [jnp.where(n < tiles, 0.0, -1e30) for n in (1, 2)]
+            hide.append(jnp.where(text_row < length, 0.0, -1e30))
+            o_parts, dq_parts = [], []
             for h in range(2):
-                keep = lane_q if h == 0 else jnp.logical_not(lane_q)
-                q_h = jnp.where(keep, q, jnp.zeros_like(q))
-                do_h = jnp.where(keep, do, jnp.zeros_like(do))
-                scores = lax.dot_general(k, q_h, contract_lanes, preferred_element_type=f32) + bias
+                scores = lax.dot_general(k, half(q, h), contract_lanes, preferred_element_type=f32)
+                scores = jnp.concatenate(
+                    [scores[n * TILE : (n + 1) * TILE] + hide[n] for n in range(4)], axis=0
+                )
                 weights = jnp.exp(scores - jnp.max(scores, axis=0, keepdims=True))
                 probs = weights * (1.0 / jnp.sum(weights, axis=0, keepdims=True))
-                dprobs = lax.dot_general(v, do_h, contract_lanes, preferred_element_type=f32)
+                dprobs = lax.dot_general(v, half(do, h), contract_lanes, preferred_element_type=f32)
                 total = jnp.sum(probs * dprobs, axis=0, keepdims=True)
-                dscores = (probs * (dprobs - total)).astype(jnp.bfloat16)
-                low = probs.astype(jnp.bfloat16)
+                dscores = (probs * (dprobs - total)).astype(bf16)
+                low = probs.astype(bf16)
+                for n in range(4):
+                    ps[r, h, n] = low[n * TILE : (n + 1) * TILE]
+                    ds[r, h, n] = dscores[n * TILE : (n + 1) * TILE]
                 span = slice(h * HEAD_DIM, (h + 1) * HEAD_DIM)
-                o_parts.append(jnp.dot(v_t[span], low, preferred_element_type=f32))
-                dq_parts.append(jnp.dot(k_t[span], dscores, preferred_element_type=f32))
-                dk_parts.append(jnp.dot(dscores, q, preferred_element_type=f32))
-                dv_parts.append(jnp.dot(low, do, preferred_element_type=f32))
-            o = jnp.concatenate(o_parts, axis=0).T.astype(jnp.bfloat16)
-            dq = (jnp.concatenate(dq_parts, axis=0).T * HEAD_DIM**-0.5).astype(jnp.bfloat16)
-            dk = jnp.where(lane_k, dk_parts[0], dk_parts[1])
-            dv = jnp.where(lane_k, dv_parts[0], dv_parts[1])
-            for j in range(3):
-                rows = slice(j * TILE, (j + 1) * TILE)
-                res[ty, i * 3 + j, 0] = o[rows]
-                res[ty, i * 3 + j, 1] = dq[rows]
-                res[ty, i * 3 + j, 2] = dk[rows].astype(jnp.bfloat16)
-                res[ty, i * 3 + j, 3] = dv[rows].astype(jnp.bfloat16)
-            dk_text, dv_text = dk[rows_q:], dv[rows_q:]
-
-            def spread(c, inner):
-                hit = jnp.where(caption == c, 1.0, 0.0)
-                tsend[ty, c, 0] += dk_text * hit
-                tsend[ty, c, 1] += dv_text * hit
-                return inner
-
-            lax.fori_loop(0, peers_grp, spread, 0)
+                o_parts.append(jnp.dot(vt[i, span, :], low, preferred_element_type=f32))
+                dq_parts.append(jnp.dot(kt[i, span, :], dscores, preferred_element_type=f32))
+            o = jnp.concatenate(o_parts, axis=0).T
+            dq = jnp.concatenate(dq_parts, axis=0).T * scale
+            res[par, ty, r, 0] = o.astype(bf16)
+            res[par, ty, r, 1] = dq.astype(bf16)
             return carry
 
-        lax.fori_loop(0, 3, image, 0)
-
-    def work(pair):
-        par = lax.rem(pair, 2)
-        for copy in caption_messages(pair):
-            copy.wait()
-
+        lax.fori_loop(0, 6, query, 0)
+
+        def key_grads(i, block):
+            begin_i = begin_of(i)
+            rows = [jnp.minimum(begin_i + n, 5) for n in range(3)]
+            q, do = qm[i], dm[i]
+            dk, dv = [], []
+            for h in range(2):
+                low = jnp.concatenate([ps[r, h, block] for r in rows], axis=1)
+                dscores = jnp.concatenate([ds[r, h, block] for r in rows], axis=1)
+                dk.append(jnp.dot(dscores, q, preferred_element_type=f32))
+                dv.append(jnp.dot(low, do, preferred_element_type=f32))
+            return jnp.where(lane, dk[0], dk[1]), jnp.where(lane, dv[0], dv[1])
+
+        def key(r, carry):
+            i = jnp.where(r >= first, 1, 0) + jnp.where(r >= second, 1, 0)
+            dk, dv = key_grads(i, jnp.minimum(r - begin_of(i), 2))
+            res[par, ty, r, 2] = dk.astype(bf16)
+            res[par, ty, r, 3] = dv.astype(bf16)
+            return carry
+
+        lax.fori_loop(0, 6, key, 0)
+
+        def caption_key(i, carry):
+            dk, dv = key_grads(i, 3)
+            tgrad[i, 0] = dk
+            tgrad[i, 1] = dv
+            return carry
+
+        lax.fori_loop(0, 3, caption_key, 0)
+
+        def spread(c, a):
+            hits = [jnp.where(mine[0, T_CAPTION + i] == c, 1.0, 0.0) for i in range(3)]
+            return tgrad[0, a] * hits[0] + tgrad[1, a] * hits[1] + tgrad[2, a] * hits[2]
+
+        def settle(c, carry):
+            for a in range(2):
+                tsend[ty, c, a] = spread(c, a).astype(bf16)
+            return carry
+
+        lax.fori_loop(0, peers_grp, settle, 0)
+        for a in range(2):
+            tself[ty, a] = spread(g, a)
+
+    def captions_in(pair, ty):
         def current(c, carry):
             for a in range(2):
-                for ty in range(2):
-                    txt[ty, a, c] = caps[pair, c, a, :, ty * LANES : (ty + 1) * LANES]
+                txt[a, c] = caps[pair, c, a, :, ty * LANES : (ty + 1) * LANES]
             return carry
 
         lax.fori_loop(0, peers_grp, current, 0)
-        for ty in range(2):
-            finish(0, par, ty, LATE)
-            fill_own(0, par, ty)
-            fill_arrived(0, par, ty)
-            fill_final(0, par, ty)
-            compute(ty)
-            first_send(1, par, ty)
-            for k in range(1, peers_grp):
-                text_message(par, ty, k).start()
+
+    def work(pair, ty):
+        final(0, pair, ty)
+        captions_in(pair, ty)
+        compute(pair, ty)
+        first_send(1, pair, ty)
+        for k in range(1, peers_grp):
+            text_message(lax.rem(pair, 2), ty, k).start()
 
     def home(pair):
-        par = lax.rem(pair, 2)
-
         @pl.when(pair > 0)
         def _():
             for copy in stores(pair - 1):
                 copy.wait()
 
         for ty in range(2):
-            finish(1, par, ty, LATE)
-            fill_own(1, par, ty)
-            fill_arrived(1, par, ty)
-            fill_final(1, par, ty)
+            final(1, pair, ty)
 
             def place(j, carry):
                 at = pl.ds(pl.multiple_of(j * TILE, TILE), TILE)
@@ -602,8 +686,6 @@
                 return carry
 
             lax.fori_loop(0, 6, place, 0)
-        for copy in end_messages(pair):
-            copy.wait()
         for copy in stores(pair):
             copy.start()
 
@@ -614,10 +696,11 @@
                 text_message(par, ty, k).wait()
             at = slice(ty * LANES, (ty + 1) * LANES)
             for a in range(2):
-                total = tsend[ty, g, a]
+                total = tself[ty, a]
                 for k in range(1, peers_grp):
-                    total = total + trecv[par, ty, k - 1, a]
-                ttot[par, a * TILE : (a + 1) * TILE, at] = total
+                    total = total + trecv[par, ty, k - 1, a].astype(jnp.float32)
+                tsum[a * TILE : (a + 1) * TILE, at] = total
+                ttot[par, a * TILE : (a + 1) * TILE, at] = total.astype(ttot.dtype)
         for copy in sum_messages(par):
             copy.start()
 
@@ -626,9 +709,9 @@
         for copy in sum_messages(par):
             copy.wait()
         at = pl.ds(pl.multiple_of(s * share, share), share)
-        total = ttot[par, at, :]
+        total = tsum[at, :]
         for k in range(1, peers_seq):
-            total = total + tpart[par, k - 1]
+            total = total + tpart[par, k - 1].astype(jnp.float32)
         done = total.astype(tdone.dtype)
         tdone[pair] = done
         tall[pair, at, :] = done
@@ -656,7 +739,7 @@
     for copy in loads(0):
         copy.wait()
     for ty in range(2):
-        first_send(0, 0, ty, plan_own)
+        first_send(0, jnp.int32(0), ty, plan_own)
     for pair in range(pairs):
         for copy in caption_messages(pair):
             copy.start()
@@ -664,63 +747,97 @@
         copy.wait()
     publish(make_plan(tab_seq[:, 0, :], mine, tab_grp[:, 0, :], s), plan)
 
+    for copy in loads(1):
+        copy.start()
+
     def superstep(step, carry):
         entering = step < pairs
         working = (step >= 1) & (step <= pairs)
-        par_in = lax.rem(step, 2)
-        par_out = lax.rem(step + 1, 2)
-
-        @pl.when(step >= 2)
-        def _():
-            home(step - 2)
-
-        @pl.when(entering & (step > 0))
-        def _():
-            for copy in loads(step):
+        leaving = step >= 2
+
+        def following():
+            for copy in loads(step + 1):
                 copy.wait()
             for ty in range(2):
-                first_send(0, par_in, ty)
+                first_send(0, step + 1, ty)
+
+        @pl.when(leaving)
+        def _():
+            turn(1, step - 2)
 
         @pl.when(working)
         def _():
-            work(step - 1)
-
-        @pl.when(step + 1 < pairs)
+            for copy in caption_messages(step - 1):
+                copy.wait()
+            work(step - 1, 0)
+
+        @pl.when(entering)
+        def _():
+            pass_on(0, step)
+
+        @pl.when(leaving)
+        def _():
+            last_send(1, step - 2)
+
+        @pl.when(working)
+        def _():
+            work(step - 1, 1)
+
+        @pl.when(leaving)
+        def _():
+            end_captions(step - 2)
+
+        @pl.when((step >= 1) & (step + 1 < pairs))
         def _():
             for copy in loads(step + 1):
                 copy.start()
 
         @pl.when(working)
         def _():
-            pass_on(1, par_out)
+            pass_on(1, step - 1)
+
+        @pl.when(entering)
+        def _():
+            turn(0, step)
+
+        @pl.when(step == 0)
+        def _():
+            following()
+
+        @pl.when(leaving)
+        def _():
+            home(step - 2)
+
+        @pl.when(entering)
+        def _():
+            last_send(0, step)
+
+        @pl.when(working)
+        def _():
             add_captions(step - 1)
 
-        @pl.when(entering)
-        def _():
-            pass_on(0, par_in)
-
-        @pl.when(working)
-        def _():
-            turn(1, par_out)
-
-        @pl.when(entering)
-        def _():
-            turn(0, par_in)
-
-        @pl.when(working)
-        def _():
-            last_send(1, par_out)
-            end_captions(step - 1)
-
-        @pl.when(entering)
-        def _():
-            last_send(0, par_in)
+        @pl.when((step >= 1) & (step + 1 < pairs))
+        def _():
+            following()
 
         return carry
 
     lax.fori_loop(0, pairs + 2, superstep, 0)
+    for pair in range(pairs):
+        for copy in end_messages(pair):
+            copy.wait()
+    for copy in caption_stores():
+        copy.start()
     for copy in stores(pairs - 1):
         copy.wait()
+    for copy in caption_stores():
+        copy.wait()
+
+
+def copy_kernel(*refs):
+    count = len(refs) // 2
+    for source, target in zip(refs[:count], refs[count:]):
+        target[...] = source[...]
 
 
 def body(
@@ -760,25 +877,36 @@
         pltpu.SMEM((8, 2 * P_SIZE), jnp.int32),
         pltpu.VMEM((2, 2, 4, rows, LANES), bf16),
         pltpu.VMEM((pairs, peers_grp, 2, text_rows, 2 * LANES), bf16),
-        pltpu.VMEM((2, 2, peers_grp, text_rows, LANES), bf16),
+        pltpu.VMEM((2, peers_grp, text_rows, LANES), bf16),
         pltpu.VMEM((2, 2, 2, SLOTS) + quad, bf16),
-        pltpu.VMEM((2, 2, 2, 2, SLOTS) + quad, bf16),
-        pltpu.VMEM((2, 2, 2, 2, RELAY) + quad, bf16),
+        pltpu.VMEM((2 + pairs, 2, 2, SLOTS) + quad, bf16),
+        pltpu.VMEM((2 + pairs, 2, 2, RELAY) + quad, bf16),
         pltpu.VMEM((2, 2, 2, SLOTS) + quad, bf16),
-        pltpu.VMEM((2, 2, 2, 2, SLOTS) + quad, bf16),
+        pltpu.VMEM((4, 2, 2, SLOTS) + quad, bf16),
         pltpu.VMEM((2, 2, 2, RELAY) + quad, bf16),
-        pltpu.VMEM((2, 2, 2, 2, RELAY) + quad, bf16),
+        pltpu.VMEM((4, 2, 2, RELAY) + quad, bf16),
         pltpu.VMEM((POOL,) + quad, bf16),
-        pltpu.VMEM((2, 9) + quad, bf16),
+        pltpu.VMEM((2, 2, 6) + quad, bf16),
         pltpu.VMEM((2, 4, rows, LANES), bf16),
-        pltpu.VMEM((2, peers_grp, 2, text_rows, LANES), f32),
-        pltpu.VMEM((2, 2, peers_grp - 1, 2, text_rows, LANES), f32),
-        pltpu.VMEM((2, 2 * text_rows, 2 * LANES), f32),
-        pltpu.VMEM((2, peers_seq - 1, 2 * text_rows // peers_seq, 2 * LANES), f32),
+        pltpu.VMEM((3, 4 * TILE, LANES), bf16),
+        pltpu.VMEM((3, 4 * TILE, LANES), bf16),
+        pltpu.VMEM((3, LANES, 4 * TILE), bf16),
+        pltpu.VMEM((3, LANES, 4 * TILE), bf16),
+        pltpu.VMEM((3, 3 * TILE, LANES), bf16),
+        pltpu.VMEM((3, 3 * TILE, LANES), bf16),
+        pltpu.VMEM((6, 2, 4, TILE, TILE), bf16),
+        pltpu.VMEM((6, 2, 4, TILE, TILE), bf16),
+        pltpu.VMEM((3, 2, TILE, LANES), f32),
+        pltpu.VMEM((2, 2, text_rows, LANES), f32),
+        pltpu.VMEM((2, peers_grp, 2, text_rows, LANES), bf16),
+        pltpu.VMEM((2, 2, peers_grp - 1, 2, text_rows, LANES), bf16),
+        pltpu.VMEM((2 * text_rows, 2 * LANES), f32),
+        pltpu.VMEM((2, 2 * text_rows, 2 * LANES), bf16),
+        pltpu.VMEM((2, peers_seq - 1, 2 * text_rows // peers_seq, 2 * LANES), bf16),
         pltpu.VMEM((pairs, 2 * text_rows // peers_seq, 2 * LANES), bf16),
         pltpu.VMEM((pairs, 2 * text_rows, 2 * LANES), bf16),
-        dma((64,)),
-        dma((64,)),
+        dma((4 * (2 + pairs) * KINDS,)),
+        dma((4 * (2 + pairs) * KINDS,)),
         dma((peers_seq + peers_grp - 2,)),
         dma((peers_seq + peers_grp - 2,)),
         dma((pairs * 2 * (peers_grp - 1),)),
@@ -790,10 +918,10 @@
         dma((pairs * (peers_seq - 1),)),
         dma((pairs * (peers_seq - 1),)),
         dma((8 + 2 * pairs,)),
-        dma((10,)),
+        dma((8 + 2 * pairs,)),
         dma,
     ]
-    return pl.pallas_call(
+    results = pl.pallas_call(
         functools.partial(main_kernel, peers_grp, peers_seq, pairs),
         out_shape=(image, image, image, image, caption, caption),
         in_specs=[smem, vmem] + [anywhere] * 6,
@@ -804,6 +932,20 @@
         ),
         name="attend",
     )(mine, mine, image_queries, image_keys, image_values, cotangent, text_keys, text_values)
+    steps = 4
+    blocks = [
+        pl.BlockSpec((rows // steps, width), lambda i: (i, 0)),
+        pl.BlockSpec((1, text_rows // steps, width), lambda i: (0, i, 0)),
+    ]
+    specs = [blocks[0]] * 4 + [blocks[1]] * 2
+    return pl.pallas_call(
+        copy_kernel,
+        grid=(steps,),
+        out_shape=(image, image, image, image, caption, caption),
+        in_specs=specs,
+        out_specs=tuple(specs),
+        name="results",
+    )(*results)
 
 
 def solution(mesh):

time: 278 us -> 258 us (0.928)
  Pallas kernels: 266 us -> 255 us
  local copies, waits for them, and re-layouts: 9.7 us -> 1.38 us
    pallas_call x1, Pallas kernels: 266 us -> 250 us  [body(): pl.pallas_call(functools.partial(main_kernel, peers_grp, peers_seq, pairs...]
    unnamed x16 -> x0, local copies, waits for them, and re-layouts: 8.32 us -> none
    pallas_call x0 -> x1, Pallas kernels: none -> 5.1 us  [body(): pl.pallas_call(copy_kernel, grid=(steps,), out_shape=(image, image, image...]
where the time goes in v3:
time: 258 us
  Pallas kernels  255 us (99%)
    pallas_call x1, Pallas kernels, body(): pl.pallas_call(functools.partial(main_kernel, peers_grp, peers_seq, pairs...  250 us

profile of v3, /device:TPU:0, one launch (start us, length us, event | category | flops | bytes accessed | tf_op | source)
XLA Modules:
  0.0 258.1 jit_solution(3949312966699091669)
XLA Ops:
  1.3 0.8 concatenate.3
  2.1 0.6 broadcast_in_dim.2.mine.mine_rows
  2.7 250.4 %attend.1 = (bf16[768,768]{1,0:T(8,128)(2,1)}, bf16[768,768]{1,0:T(8,128)(2,1)}, bf16[768,768]{1,0:T(8,128)(2,1)}, bf16[768,768]{1,0:T(8,128)(2,1)}, bf16[1,128,...) custom-call(s32[8,128]{1,0:T(8,128)} %broadcast_in_dim.2.mine.mine_rows, s32[8,128]{1,0:T(8,128)} %broadcast_in_dim.2.mine.mine_rows, ...), custom_call_target="tpu_custom_call" | custom-call | tf_op jit(solution)/shard_map/attend/pallas_call | solution.py:924
  253.0 5.1 %results.1 = (bf16[768,768]{1,0:T(8,128)(2,1)}, bf16[768,768]{1,0:T(8,128)(2,1)}, bf16[768,768]{1,0:T(8,128)(2,1)}, bf16[768,768]{1,0:T(8,128)(2,1)}, bf16[1,128...) custom-call(bf16[768,768]{1,0:T(8,128)(2,1)} %get-tuple-element.12.refs_0_, bf16[768,768]{1,0:T(8,128)(2,1)} %get-tuple-element.13.refs_1_, ...), custom_call_target="tpu_custom_call" | custom-call | tf_op jit(solution)/shard_map/results/pallas_call | solution.py:941
  (1 shorter events, 0.0 us)

commit v4 on v3

--- a/solution.py
+++ b/solution.py
@@ -513,6 +513,11 @@
         for ty in range(2):
             finish(io, pair, ty, SEND_NEAR)
             finish(io, pair, ty, PASS)
+            if io == 0 and ty == 1:
+                @pl.when(pair > 0)
+                def _():
+                    sent(pair - 1)
+
             fill_own(io, pair, ty)
             fill_arrived(io, pair, ty)
             entry = P_BACK_MID if io else P_MID
@@ -530,8 +535,16 @@
             choose(send_l, io, ty, P_BACK_LATE if io else P_LATE, RELAY, 0, RELAY)
             begin(io, pair, ty, LATE)
 
+    def sent(pair):
+        for sign in range(2):
+            message(0, pair, 1, sign, MID_NEAR).wait_send()
+
     def final(io, pair, ty):
-        finish(io, pair, ty, MID_NEAR)
+        if io == 0 and ty == 1:
+            for sign in range(2):
+                message(io, pair, ty, sign, MID_NEAR).wait_recv()
+        else:
+            finish(io, pair, ty, MID_NEAR)
         finish(io, pair, ty, LATE)
         fill_own(io, pair, ty)
         fill_arrived(io, pair, ty)
@@ -610,7 +623,11 @@
             res[par, ty, r, 1] = dq.astype(bf16)
             return carry
 
-        lax.fori_loop(0, 6, query, 0)
+        def query_two(r, carry):
+            query(2 * r, carry)
+            return query(2 * r + 1, carry)
+
+        lax.fori_loop(0, 3, query_two, 0)
 
         def key_grads(i, block):
             begin_i = begin_of(i)
@@ -761,9 +778,9 @@
             for ty in range(2):
                 first_send(0, step + 1, ty)
 
-        @pl.when(leaving)
-        def _():
-            turn(1, step - 2)
+        @pl.when(entering)
+        def _():
+            pass_on(0, step)
 
         @pl.when(working)
         def _():
@@ -773,7 +790,7 @@
 
         @pl.when(entering)
         def _():
-            pass_on(0, step)
+            turn(0, step)
 
         @pl.when(leaving)
         def _():
@@ -782,6 +799,14 @@
         @pl.when(working)
         def _():
             work(step - 1, 1)
+
+        @pl.when(working)
+        def _():
+            pass_on(1, step - 1)
+
+        @pl.when(entering)
+        def _():
+            last_send(0, step)
 
         @pl.when(leaving)
         def _():
@@ -792,29 +817,21 @@
             for copy in loads(step + 1):
                 copy.start()
 
+        @pl.when(leaving)
+        def _():
+            home(step - 2)
+
         @pl.when(working)
         def _():
-            pass_on(1, step - 1)
-
-        @pl.when(entering)
-        def _():
-            turn(0, step)
+            add_captions(step - 1)
 
         @pl.when(step == 0)
         def _():
             following()
 
-        @pl.when(leaving)
-        def _():
-            home(step - 2)
-
-        @pl.when(entering)
-        def _():
-            last_send(0, step)
-
         @pl.when(working)
         def _():
-            add_captions(step - 1)
+            turn(1, step - 1)
 
         @pl.when((step >= 1) & (step + 1 < pairs))
         def _():
@@ -823,6 +840,7 @@
         return carry
 
     lax.fori_loop(0, pairs + 2, superstep, 0)
+    sent(pairs - 1)
     for pair in range(pairs):
         for copy in end_messages(pair):
             copy.wait()

time: 258 us -> 244 us (0.946)
  Pallas kernels: 255 us -> 242 us
    pallas_call x1, Pallas kernels: 250 us -> 236 us  [body(): pl.pallas_call(functools.partial(main_kernel, peers_grp, peers_seq, pairs...]
where the time goes in v4:
time: 244 us
  Pallas kernels  242 us (99%)
    pallas_call x1, Pallas kernels, body(): pl.pallas_call(functools.partial(main_kernel, peers_grp, peers_seq, pairs...  236 us
    pallas_call x1, Pallas kernels, body(): pl.pallas_call(copy_kernel, grid=(steps,), out_shape=(image, image, image...  5.1 us

profile of v4, /device:TPU:0, one launch (start us, length us, event | category | flops | bytes accessed | tf_op | source)
XLA Modules:
  0.0 244.2 jit_solution(17468803334476018839)
XLA Ops:
  1.3 0.8 concatenate.3
  2.1 0.6 broadcast_in_dim.2.mine.mine_rows
  2.7 236.5 %attend.1 = (bf16[768,768]{1,0:T(8,128)(2,1)}, bf16[768,768]{1,0:T(8,128)(2,1)}, bf16[768,768]{1,0:T(8,128)(2,1)}, bf16[768,768]{1,0:T(8,128)(2,1)}, bf16[1,128,...) custom-call(s32[8,128]{1,0:T(8,128)} %broadcast_in_dim.2.mine.mine_rows, s32[8,128]{1,0:T(8,128)} %broadcast_in_dim.2.mine.mine_rows, ...), custom_call_target="tpu_custom_call" | custom-call | tf_op jit(solution)/shard_map/attend/pallas_call | solution.py:942
  239.1 5.1 %results.1 = (bf16[768,768]{1,0:T(8,128)(2,1)}, bf16[768,768]{1,0:T(8,128)(2,1)}, bf16[768,768]{1,0:T(8,128)(2,1)}, bf16[768,768]{1,0:T(8,128)(2,1)}, bf16[1,128...) custom-call(bf16[768,768]{1,0:T(8,128)(2,1)} %get-tuple-element.12.refs_0_, bf16[768,768]{1,0:T(8,128)(2,1)} %get-tuple-element.13.refs_1_, ...), custom_call_target="tpu_custom_call" | custom-call | tf_op jit(solution)/shard_map/results/pallas_call | solution.py:959
  (1 shorter events, 0.0 us)

commit v5 on v4

--- a/solution.py
+++ b/solution.py
@@ -439,10 +439,11 @@
 
     def fill(base, count, read):
         def step(k, carry):
-            pool[base + k] = read(k)
+            pool[base + 2 * k] = read(2 * k)
+            pool[base + 2 * k + 1] = read(2 * k + 1)
             return carry
 
-        lax.fori_loop(0, count, step, 0)
+        lax.fori_loop(0, count // 2, step, 0)
 
     def fill_own(io, pair, ty):
         par = lax.rem(pair, 2)
@@ -623,11 +624,12 @@
             res[par, ty, r, 1] = dq.astype(bf16)
             return carry
 
-        def query_two(r, carry):
-            query(2 * r, carry)
-            return query(2 * r + 1, carry)
-
-        lax.fori_loop(0, 3, query_two, 0)
+        def query_three(r, carry):
+            query(3 * r, carry)
+            query(3 * r + 1, carry)
+            return query(3 * r + 2, carry)
+
+        lax.fori_loop(0, 2, query_three, 0)
 
         def key_grads(i, block):
             begin_i = begin_of(i)
@@ -648,7 +650,11 @@
             res[par, ty, r, 3] = dv.astype(bf16)
             return carry
 
-        lax.fori_loop(0, 6, key, 0)
+        def key_two(r, carry):
+            key(2 * r, carry)
+            return key(2 * r + 1, carry)
+
+        lax.fori_loop(0, 3, key_two, 0)
 
         def caption_key(i, carry):
             dk, dv = key_grads(i, 3)
@@ -950,7 +956,7 @@
         ),
         name="attend",
     )(mine, mine, image_queries, image_keys, image_values, cotangent, text_keys, text_values)
-    steps = 4
+    steps = 2
     blocks = [
         pl.BlockSpec((rows // steps, width), lambda i: (i, 0)),
         pl.BlockSpec((1, text_rows // steps, width), lambda i: (0, i, 0)),

time: 244 us -> 242 us (level)
  Pallas kernels: 242 us -> 239 us
where the time goes in v5:
time: 242 us
  Pallas kernels  239 us (99%)
    pallas_call x1, Pallas kernels, body(): pl.pallas_call(functools.partial(main_kernel, peers_grp, peers_seq, pairs...  235 us

profile of v5, /device:TPU:0, one launch (start us, length us, event | category | flops | bytes accessed | tf_op | source)
XLA Modules:
  0.0 242.1 jit_solution(16289719074019977912)
XLA Ops:
  1.3 0.8 concatenate.3
  2.1 0.6 broadcast_in_dim.2.mine.mine_rows
  2.7 235.4 %attend.1 = (bf16[768,768]{1,0:T(8,128)(2,1)}, bf16[768,768]{1,0:T(8,128)(2,1)}, bf16[768,768]{1,0:T(8,128)(2,1)}, bf16[768,768]{1,0:T(8,128)(2,1)}, bf16[1,128,...) custom-call(s32[8,128]{1,0:T(8,128)} %broadcast_in_dim.2.mine.mine_rows, s32[8,128]{1,0:T(8,128)} %broadcast_in_dim.2.mine.mine_rows, ...), custom_call_target="tpu_custom_call" | custom-call | tf_op jit(solution)/shard_map/attend/pallas_call | solution.py:948
  238.0 4.1 %results.1 = (bf16[768,768]{1,0:T(8,128)(2,1)}, bf16[768,768]{1,0:T(8,128)(2,1)}, bf16[768,768]{1,0:T(8,128)(2,1)}, bf16[768,768]{1,0:T(8,128)(2,1)}, bf16[1,128...) custom-call(bf16[768,768]{1,0:T(8,128)(2,1)} %get-tuple-element.12.refs_0_, bf16[768,768]{1,0:T(8,128)(2,1)} %get-tuple-element.13.refs_1_, ...), custom_call_target="tpu_custom_call" | custom-call | tf_op jit(solution)/shard_map/results/pallas_call | solution.py:965
  (1 shorter events, 0.0 us)

commit v6 on v5

--- a/solution.py
+++ b/solution.py
@@ -784,6 +784,10 @@
             for ty in range(2):
                 first_send(0, step + 1, ty)
 
+        @pl.when(step > pairs)
+        def _():
+            end_captions(pairs - 1)
+
         @pl.when(entering)
         def _():
             pass_on(0, step)
@@ -814,7 +818,7 @@
         def _():
             last_send(0, step)
 
-        @pl.when(leaving)
+        @pl.when(leaving & (step <= pairs))
         def _():
             end_captions(step - 2)
 

time: 242 us -> 242 us (level)
  no operation moved by 1% of the time
where the time goes in v6:
time: 242 us
  Pallas kernels  240 us (99%)
    pallas_call x1, Pallas kernels, body(): pl.pallas_call(functools.partial(main_kernel, peers_grp, peers_seq, pairs...  235 us

profile of v6, /device:TPU:0, one launch (start us, length us, event | category | flops | bytes accessed | tf_op | source)
XLA Modules:
  0.0 242.2 jit_solution(9427536267606585346)
XLA Ops:
  1.3 0.8 concatenate.3
  2.1 0.6 broadcast_in_dim.2.mine.mine_rows
  2.7 235.4 %attend.1 = (bf16[768,768]{1,0:T(8,128)(2,1)}, bf16[768,768]{1,0:T(8,128)(2,1)}, bf16[768,768]{1,0:T(8,128)(2,1)}, bf16[768,768]{1,0:T(8,128)(2,1)}, bf16[1,128,...) custom-call(s32[8,128]{1,0:T(8,128)} %broadcast_in_dim.2.mine.mine_rows, s32[8,128]{1,0:T(8,128)} %broadcast_in_dim.2.mine.mine_rows, ...), custom_call_target="tpu_custom_call" | custom-call | tf_op jit(solution)/shard_map/attend/pallas_call | solution.py:952
  238.1 4.1 %results.1 = (bf16[768,768]{1,0:T(8,128)(2,1)}, bf16[768,768]{1,0:T(8,128)(2,1)}, bf16[768,768]{1,0:T(8,128)(2,1)}, bf16[768,768]{1,0:T(8,128)(2,1)}, bf16[1,128...) custom-call(bf16[768,768]{1,0:T(8,128)(2,1)} %get-tuple-element.12.refs_0_, bf16[768,768]{1,0:T(8,128)(2,1)} %get-tuple-element.13.refs_1_, ...), custom_call_target="tpu_custom_call" | custom-call | tf_op jit(solution)/shard_map/results/pallas_call | solution.py:969
  (1 shorter events, 0.0 us)
